TPU v7x, 32 devices: a whole 2x2x4 slice. The times are simulated.
32 devices in a mesh: section: 4 (over x, core), dp: 8 (over z, y).
Axes of the slice: x: 2, y: 2, z: 4, core: 2. Of those that a mesh axis runs over, the one named last changes fastest.
Arguments:
- value_weight: bfloat16 [4, 8192, 1024], P('section', 'dp'), may hold values from -0.0625 to 0.0625
- norm_gain: bfloat16 [4, 8192], P('section'), may hold values from 0.25 to 1.75
- mask_logits: bfloat16 [4, 6, 2048, 1024], P('section', None, 'dp'), may hold values from -5 to 5
- gumbel_noise: bfloat16 [4, 6, 2048, 1024], P('section', None, 'dp'), may hold values from -2.23 to 9.22, as said below
- stream_in: bfloat16 [2, 512, 8192], P(None, 'dp'), may hold values from -6 to 6
- stream_grad: bfloat16 [2, 512, 8192], P(None, 'dp'), may hold values from -6 to 6
Outputs:
- logit_grad: bfloat16 [4, 6, 2048, 1024], P('section', None, 'dp')
Inputs may be any that keep to these rules, and one draw needn't show every extreme that they name: `gumbel_noise`: gumbel noise, minus the log of minus the log of a uniform number.
All inputs are finite; a program needn't handle non-finite values.
Results may differ from a plain program's by a relative error of at most 0.029.
Values may be sent and summed in bfloat16 or wider, within the bound.
A program may use at most 128 MiB of HBM per device.

v0:
```python
import jax
import jax.numpy as jnp
from jax import lax
from jax.sharding import PartitionSpec as P

VHEADS = 8


sharpness_divisor = 0.6666667
epsilon = 1e-05


def shifted(x, axis, by):
    count = lax.axis_size(axis)
    pairs = [(i, i + by) for i in range(count) if 0 <= i + by < count]
    return lax.ppermute(x, axis, pairs)


def soft_mask(keeping_propensity, perturbed_draw):
    ranking_measure = (
        keeping_propensity.astype(jnp.float32) + perturbed_draw.astype(jnp.float32)
    ) / sharpness_divisor
    expo = jnp.exp(ranking_measure)
    probs = expo / jnp.sum(expo, axis=0)
    first = probs[0] + probs[1] + probs[2]
    second = probs[0] + probs[3] + probs[4]
    third = probs[1] + probs[3] + probs[5]
    fourth = probs[2] + probs[4] + probs[5]
    mask = jnp.stack([first, second, third, fourth], axis=1)
    return (probs, mask.reshape(-1, mask.shape[-1]))


def mask_logit_backward(probs, weight, grads):
    dmask = (grads * weight.astype(jnp.float32)).reshape(-1, 4, grads.shape[-1])
    row_a, row_b, row_c, row_d = (dmask[:, 0], dmask[:, 1], dmask[:, 2], dmask[:, 3])
    dprob = jnp.stack(
        [row_a + row_b, row_a + row_c, row_a + row_d, row_b + row_c, row_b + row_d, row_c + row_d]
    )
    ranking_derivative = probs * (dprob - jnp.sum(probs * dprob, axis=0))
    return (ranking_derivative / sharpness_divisor).astype(jnp.bfloat16)


def norm_forward(stream, gain):
    values = stream.astype(jnp.float32)
    scale = lax.rsqrt(jnp.mean(values * values, axis=-1, keepdims=True) + epsilon)
    normed = (values * scale * gain).astype(jnp.bfloat16)
    return (values, scale, normed)


def expand(value, width):
    count = value.shape[0]
    head = value.shape[1] // VHEADS
    repeat = width // value.shape[1]
    grown = jnp.broadcast_to(value.reshape(count, VHEADS, 1, head), (count, VHEADS, repeat, head))
    return grown.reshape(count, width)


def collapse(grad, kv_width):
    count, width = grad.shape
    head = kv_width // VHEADS
    repeat = width // kv_width
    return jnp.sum(grad.reshape(count, VHEADS, repeat, head), axis=2).reshape(count, kv_width)


def norm_backward(values, scale, gain, dnormed):
    scaled = dnormed * gain
    return scale * scaled - values * (scale * scale * scale) * jnp.mean(
        scaled * values, axis=-1, keepdims=True
    )


def keep_slot(saved, item, slot, valid):
    old = lax.dynamic_index_in_dim(saved, slot, 0, keepdims=False)
    return lax.dynamic_update_index_in_dim(saved, jnp.where(valid, item, old), slot, 0)


def send_forward(output):
    return shifted(output, "section", 1)


def send_backward(grad):
    return shifted(grad, "section", -1)


def per_device(value_weight, norm_gain, mask_logits, gumbel_noise, stream_in, stream_grad):
    section = lax.axis_index("section")
    sections = lax.axis_size("section")
    micro, rows, width = stream_in.shape
    weight = value_weight[0]
    gain = norm_gain[0].astype(jnp.float32)
    probs, mask = soft_mask(mask_logits[0], gumbel_noise[0])
    masked = (weight.astype(jnp.float32) * mask).astype(jnp.bfloat16)
    weights = lax.all_gather(masked, "dp", axis=0, tiled=True)
    kv_width = weights.shape[1]
    saved_x = jnp.zeros((micro, rows, width), jnp.bfloat16)
    saved_u = jnp.zeros((micro, rows, width), jnp.bfloat16)
    saved_g = jnp.zeros((micro, rows, kv_width), jnp.bfloat16)
    steps = micro + sections - 1
    received_state = jnp.zeros((rows, width), jnp.bfloat16)
    for step in range(steps):
        index = step - section
        valid = (index >= 0) & (index < micro)
        slot = jnp.clip(index, 0, micro - 1)
        taken = jnp.where(
            section == 0,
            lax.dynamic_index_in_dim(stream_in, slot, 0, keepdims=False),
            received_state,
        )
        values, scale, normed = norm_forward(taken, gain)
        value = jnp.dot(normed, weights, preferred_element_type=jnp.float32)
        output = (values + expand(value, width)).astype(jnp.bfloat16)
        saved_x = keep_slot(saved_x, taken, slot, valid)
        saved_u = keep_slot(saved_u, normed, slot, valid)
        if step + 1 < steps:
            received_state = send_forward(output)
    received_state = jnp.zeros((rows, width), jnp.bfloat16)
    for step in range(steps):
        index = step - (sections - 1 - section)
        valid = (index >= 0) & (index < micro)
        slot = jnp.clip(index, 0, micro - 1)
        taken = jnp.where(
            section == sections - 1,
            lax.dynamic_index_in_dim(stream_grad, slot, 0, keepdims=False),
            received_state,
        )
        upper = taken.astype(jnp.float32)
        vgrad = collapse(upper, kv_width).astype(jnp.bfloat16)
        dnormed = lax.dot_general(
            vgrad, weights, (((1,), (1,)), ((), ())), preferred_element_type=jnp.float32
        )
        values, scale, normed = norm_forward(
            lax.dynamic_index_in_dim(saved_x, slot, 0, keepdims=False), gain
        )
        lower = (upper + norm_backward(values, scale, gain, dnormed)).astype(jnp.bfloat16)
        saved_g = keep_slot(saved_g, vgrad, slot, valid)
        if step + 1 < steps:
            received_state = send_backward(lower)
    flat_u = saved_u.reshape(micro * rows, width)
    flat_g = saved_g.reshape(micro * rows, kv_width)
    spread = lax.all_to_all(flat_u, "dp", split_axis=1, concat_axis=0, tiled=True)
    block = flat_g.shape[0]
    piece = lax.all_gather(flat_g, "dp", axis=0, tiled=True)
    count = piece.shape[0]
    pieces = count // block
    left = spread.reshape(pieces, block, spread.shape[1])
    right = piece.reshape(pieces, block, kv_width)
    terms = jnp.einsum("brf,brk->bfk", left, right, preferred_element_type=jnp.float32)
    rounded = lax.optimization_barrier(terms.astype(jnp.bfloat16))
    wgrad = jnp.sum(rounded.astype(jnp.float32), axis=0)
    return mask_logit_backward(probs, weight, wgrad)[None]


def solution(mesh):
    return jax.shard_map(
        per_device,
        mesh=mesh,
        in_specs=(
            P("section", "dp", None),
            P("section", None),
            P("section", None, "dp", None),
            P("section", None, "dp", None),
            P(None, "dp", None),
            P(None, "dp", None),
        ),
        out_specs=P("section", None, "dp", None),
        check_vma=False,
    )
```

profile of v0, /device:TPU:0, one launch (start us, length us, event | category | flops | bytes accessed | tf_op | source)
XLA Modules:
  0.0 770.2 jit_solution(5094980246493383239)
XLA Ops:
  6.5 10.7 %fusion = f32[256,1024]{1,0:T(8,128)S(1)} fusion(bf16[1,6,256,1024]{3,2,1,0:T(8,128)(2,1)} %param.9, bf16[1,6,256,1024]{3,2,1,0:T(8,128)(2,1)} %param.8), kind=kLoop, calls=%fused_computation.10 | loop fusion | flops 7602176 | bytes 7340032 | tf_op jit(solution)/shard_map/reduce_sum | solution.py:24
  18.3 19.8 %bitcast_divide_fusion = f32[6,256,1024]{2,0,1:T(8,128)} fusion(bf16[1,6,256,1024]{3,2,1,0:T(8,128)(2,1)S(1)} %copy-done, bf16[1,6,256,1024]{3,2,1,0:T(8,128)(2,1)S(1)} %copy-done.2, f32[256,1024]{1,0:T(8,128)S(1)} %fusion), kind=kLoop, calls=%fused_computation.6 | loop fusion | flops 7864320 | bytes 13631488 | tf_op jit(solution)/shard_map/div | solution.py:24
  38.0 23.8 %add_bitcast_fusion.3 = (f32[256,1,1024]{2,1,0:T(1,128)S(1)}, f32[256,1,1024]{2,1,0:T(1,128)S(1)}, f32[256,1,1024]{2,1,0:T(1,128)S(1)}, f32[256,1,1024]{2,1,0:T(1,128)}) fusion(f32[6,256,1024]{2,0,1:T(8,128)} %bitcast_divide_fusion), kind=kLoop, calls=%fused_computation.124 | loop fusion | flops 2097152 | bytes 10485760 | tf_op jit(solution)/shard_map/add | solution.py:25
  61.8 6.4 pad_maximum_fusion
  68.2 5.4 reshape.654
  73.6 4.3 fusion.1
  84.3 224.1 %all-gather.3.cloned.1.call-done = bf16[8192,1024]{1,0:T(8,128)(2,1)} async-done(((bf16[1024,1024]{1,0:T(8,128)(2,1)}), bf16[8192,1024]{1,0:T(8,128)(2,1)}) %all-gather.3.cloned.1.call-update) | async-done | bytes 16777232 | tf_op jit(solution)/shard_map/all_gather | solution.py:93
  308.4 20.7 %copy.12 = bf16[1024,8192]{1,0:T(8,128)(2,1)} copy(bf16[1024,8192]{0,1:T(8,128)(2,1)} %bitcast.257) | data formatting | bytes 33554432 | tf_op jit(solution)/shard_map/dot_general | solution.py:110
  329.2 9.2 %fusion.49 = f32[64,8,128]{2,0,1:T(8,128)S(1)} fusion(bf16[8,128,8192]{2,1,0:T(8,128)(2,1)} %bitcast.260, f32[8192]{0:T(1024)S(1)} %bitcast.274, f32[64]{0:T(128)S(1)} %add_rsqrt_fusion.8, bf16[2,64,8192]{2,1,0:T(8,128)(2,1)} %param.10, s32[]{:T(128)S(6)} %min.31, pred[]{:T(512)S(6)} %eq.4), kind=kOutput, calls=%fused_computation.116 | convolution fusion | flops 1076363264 | bytes 18120964 | tf_op jit(solution)/shard_map/dot_general | solution.py:110
  339.9 2.2 fusion.5
  342.1 2.4 collective-permute-start
  347.3 9.0 %convolution_bitcast_fusion.2 = f32[8,8,8,128]{3,1,2,0:T(8,128)S(1)} fusion(bf16[8192,1024]{1,0:T(8,128)(2,1)} %all-gather.3.cloned.1.call-done, bf16[64,8192]{1,0:T(8,128)(2,1)S(1)} %get-tuple-element.17, f32[8192]{0:T(1024)S(1)} %bitcast.275, f32[64]{0:T(128)S(1)} %add_rsqrt_fusion.7), kind=kOutput, calls=%fused_computation.90 | convolution fusion | flops 1075838976 | bytes 18120960 | tf_op jit(solution)/shard_map/dot_general | solution.py:110
  358.1 14.2 %collective-permute-start.1 = (bf16[64,8192]{1,0:T(8,128)(2,1)S(1)}, bf16[64,8192]{1,0:T(8,128)(2,1)S(1)}, u32[]{:S(2)}, u32[]{:S(2)}) collective-permute-start(bf16[64,8192]{1,0:T(8,128)(2,1)S(1)} %fusion.17), channel_id=1, source_target_pairs={{0,8},{8,16},{16,24},{1,9},{9,17},{17,25},{2,10},{10,18},{18,26},{... | collective-permute-start | bytes 3145736 | tf_op jit(solution)/shard_map/ppermute | solution.py:16
  376.0 3.1 convolution_bitcast_fusion.1
  380.8 12.8 %collective-permute-start.2 = (bf16[64,8192]{1,0:T(8,128)(2,1)S(1)}, bf16[64,8192]{1,0:T(8,128)(2,1)S(1)}, u32[]{:S(2)}, u32[]{:S(2)}) collective-permute-start(bf16[64,8192]{1,0:T(8,128)(2,1)S(1)} %fusion.21), channel_id=1, source_target_pairs={{0,8},{8,16},{16,24},{1,9},{9,17},{17,25},{2,10},{10,18},{18,26},{... | collective-permute-start | bytes 3145736 | tf_op jit(solution)/shard_map/ppermute | solution.py:16
  397.2 3.1 convolution_bitcast_fusion
  402.1 13.3 %collective-permute-start.3 = (bf16[64,8192]{1,0:T(8,128)(2,1)S(1)}, bf16[64,8192]{1,0:T(8,128)(2,1)S(1)}, u32[]{:S(2)}, u32[]{:S(2)}) collective-permute-start(bf16[64,8192]{1,0:T(8,128)(2,1)S(1)} %fusion.25), channel_id=1, source_target_pairs={{0,8},{8,16},{16,24},{1,9},{9,17},{17,25},{2,10},{10,18},{18,26},{... | collective-permute-start | bytes 3145736 | tf_op jit(solution)/shard_map/ppermute | solution.py:16
  420.6 13.1 %fusion.40 = (f32[64]{0:T(128)S(1)}, f32[64]{0:T(128)S(1)}, f32[64]{0:T(128)S(1)}, f32[64]{0:T(128)S(1)}, f32[64]{0:T(128)S(1)}, /*index=5*/f32[64,8192]{1,0:T(8,128)}) fusion(bf16[2,64,8192]{2,1,0:T(8,128)(2,1)S(1)} %get-tuple-element.29, s32[]{:T(128)S(6)} %min.39, s32[]{:T(128)S(6)} %min.36, s32[]{:T(128)S(6)} %min.38, s32[]{:T(128)S(6)} %min.37, ...), kind=kOutput, calls=%fused_computation.83 | convolution fusion | flops 1081606144 | bytes 23233808 | tf_op jit(solution)/shard_map/dot_general | solution.py:128
  433.8 2.6 fusion.30
  438.2 13.1 %collective-permute-done.4 = bf16[64,8192]{1,0:T(8,128)(2,1)S(1)} collective-permute-done((bf16[64,8192]{1,0:T(8,128)(2,1)S(1)}, bf16[64,8192]{1,0:T(8,128)(2,1)S(1)}, u32[]{:S(2)}, u32[]{:S(2)}) %collective-permute-start.4) | collective-permute-done | bytes 1048608 | tf_op jit(solution)/shard_map/ppermute | solution.py:16
  452.8 1.8 reduce.4
  454.6 12.4 %fusion.35 = (f32[64]{0:T(128)S(1)}, f32[64,8192]{1,0:T(8,128)}) fusion(bf16[2,64,8192]{2,1,0:T(8,128)(2,1)S(1)} %get-tuple-element.29, s32[]{:T(128)S(6)} %min.37, f32[8192]{0:T(1024)S(1)} %bitcast.283, bf16[8192,1024]{1,0:T(8,128)(2,1)} %all-gather.3.cloned.1.call-done, bf16[8,8,8,128]{3,2,1,0:T(8,128)(2,1)S(1)} %copy.68), kind=kOutput, calls=%fused_computation.78 | convolution fusion | flops 1075838976 | bytes 20087044 | tf_op jit(solution)/shard_map/dot_general | solution.py:128
  467.1 2.7 fusion.11
  471.1 15.5 %collective-permute-done.5 = bf16[64,8192]{1,0:T(8,128)(2,1)S(1)} collective-permute-done((bf16[64,8192]{1,0:T(8,128)(2,1)S(1)}, bf16[64,8192]{1,0:T(8,128)(2,1)S(1)}, u32[]{:S(2)}, u32[]{:S(2)}) %collective-permute-start.5) | collective-permute-done | bytes 1048608 | tf_op jit(solution)/shard_map/ppermute | solution.py:16
  488.1 2.5 reduce.5
  491.5 12.4 %fusion.39 = (f32[64]{0:T(128)S(1)}, f32[64,8192]{1,0:T(8,128)}) fusion(bf16[2,64,8192]{2,1,0:T(8,128)(2,1)S(1)} %get-tuple-element.29, s32[]{:T(128)S(6)} %min.38, f32[8192]{0:T(1024)S(1)} %bitcast.284, bf16[8192,1024]{1,0:T(8,128)(2,1)} %all-gather.3.cloned.1.call-done, bf16[8,8,8,128]{3,2,1,0:T(8,128)(2,1)S(1)} %copy.69), kind=kOutput, calls=%fused_computation.82 | convolution fusion | flops 1075838976 | bytes 20087044 | tf_op jit(solution)/shard_map/dot_general | solution.py:128
  504.0 2.7 fusion.12
  508.1 14.6 %collective-permute-done.6 = bf16[64,8192]{1,0:T(8,128)(2,1)S(1)} collective-permute-done((bf16[64,8192]{1,0:T(8,128)(2,1)S(1)}, bf16[64,8192]{1,0:T(8,128)(2,1)S(1)}, u32[]{:S(2)}, u32[]{:S(2)}) %collective-permute-start.6) | collective-permute-done | bytes 1048608 | tf_op jit(solution)/shard_map/ppermute | solution.py:16
  524.3 2.5 reduce.6
  528.3 12.5 %fusion.43 = (f32[64]{0:T(128)S(1)}, f32[64,8192]{1,0:T(8,128)}) fusion(bf16[2,64,8192]{2,1,0:T(8,128)(2,1)S(1)} %get-tuple-element.29, s32[]{:T(128)S(6)} %min.39, f32[8192]{0:T(1024)S(1)} %bitcast.285, bf16[8192,1024]{1,0:T(8,128)(2,1)} %all-gather.3.cloned.1.call-done, bf16[8,8,8,128]{3,2,1,0:T(8,128)(2,1)} %copy.70), kind=kOutput, calls=%fused_computation.86 | convolution fusion | flops 1075838976 | bytes 20087044 | tf_op jit(solution)/shard_map/dot_general | solution.py:128
  540.8 3.5 fusion.13
  546.7 3.0 copy.27
  549.7 2.8 copy.14
  552.6 4.5 all-to-all-start
  557.4 3.3 collective-permute-done.7
  563.2 5.0 reshape.675
  568.2 40.7 %all-to-all-done = bf16[128,8,1024]{0,2,1:T(8,128)(2,1)} async-done(((bf16[128,8,1024]{0,2,1:T(8,128)(2,1)}), bf16[128,8,1024]{0,2,1:T(8,128)(2,1)}, u32[]{:S(2)}, u32[]{:S(2)}) %all-to-all-start) | async-done | bytes 2097184 | tf_op jit(solution)/shard_map/all_to_all | solution.py:140
  608.9 33.4 %all-gather.5.cloned.1.call-done = bf16[1024,1024]{1,0:T(8,128)(2,1)} async-done(((bf16[128,1024]{1,0:T(8,128)(2,1)}), bf16[1024,1024]{1,0:T(8,128)(2,1)}) %all-gather.5.cloned.1.call-update) | async-done | bytes 2097168 | tf_op jit(solution)/shard_map/all_gather | solution.py:142
  642.3 12.5 %convolution_convert_fusion = bf16[8,1024,1024]{2,1,0:T(8,128)(2,1)} fusion(bf16[8,128,1024]{2,1,0:T(8,128)(2,1)} %bitcast.294, bf16[128,8,1024]{0,2,1:T(8,128)(2,1)} %all-to-all-done), kind=kOutput, calls=%fused_computation.1 | convolution fusion | flops 2155872256 | bytes 20971520 | tf_op jit(solution)/shard_map/brf,brk->bfk/dot_general | solution.py:147
  654.7 9.2 %convert_reduce_fusion = f32[1024,1024]{1,0:T(8,128)} fusion(bf16[8,1024,1024]{2,1,0:T(8,128)(2,1)} %convolution_convert_fusion), kind=kLoop, calls=%fused_computation | loop fusion | flops 15728640 | bytes 20971520 | tf_op jit(solution)/shard_map/reduce_sum | solution.py:149
  663.9 5.2 reduce_sum.211
  669.1 5.5 mul.388
  674.5 7.1 slice_add_fusion
  681.6 20.9 %stack.38 = f32[6,256,1024]{2,0,1:T(8,128)} concatenate(f32[1,256,1024]{2,0,1:T(1,128)} %bitcast.269, f32[1,256,1024]{2,0,1:T(1,128)} %bitcast.267, f32[1,256,1024]{2,0,1:T(1,128)} %bitcast.265, f32[1,256,1024]{2,0,1:T(1,128)} %bitcast.271, f32[1,256,1024]{2,0,1:T(1,128)} %bitcast.263, f32[1,256,1024]{2,0,1:T(1,128)} %bitcast.261), dimensions={0} | concatenate | bytes 12582912 | tf_op jit(solution)/shard_map/stack | solution.py:36
  702.6 19.6 %multiply_reduce_fusion = f32[256,1024]{1,0:T(8,128)} fusion(f32[6,256,1024]{2,0,1:T(8,128)} %stack.38, f32[256,1024]{1,0:T(8,128)} %copy-done.12, bf16[1,6,256,1024]{3,2,1,0:T(8,128)(2,1)S(1)} %copy-done.1, bf16[1,6,256,1024]{3,2,1,0:T(8,128)(2,1)} %param.8), kind=kLoop, calls=%fused_computation.8 | loop fusion | flops 10747904 | bytes 14680064 | tf_op jit(solution)/shard_map/reduce_sum | solution.py:39
  722.2 20.8 %stack.37 = f32[1,6,256,1024]{3,1,2,0:T(8,128)} concatenate(f32[1,1,256,1024]{3,1,2,0:T(1,128)} %bitcast.270, f32[1,1,256,1024]{3,1,2,0:T(1,128)} %bitcast.268, f32[1,1,256,1024]{3,1,2,0:T(1,128)} %bitcast.266, f32[1,1,256,1024]{3,1,2,0:T(1,128)} %bitcast.272, f32[1,1,256,1024]{3,1,2,0:T(1,128)} %bitcast.264, f32[1,1,256,1024]{3,1,2,0:T(1,128)} %bitcast.262), dimensions={1} | concatenate | bytes 12582912 | tf_op jit(solution)/shard_map/stack | solution.py:36
  743.0 16.8 %multiply_convert_fusion = bf16[1,6,256,1024]{3,1,2,0:T(8,128)(2,1)S(1)} fusion(f32[1,6,256,1024]{3,1,2,0:T(8,128)} %stack.37, bf16[1,6,256,1024]{3,2,1,0:T(8,128)(2,1)S(1)} %copy-done.1, bf16[1,6,256,1024]{3,2,1,0:T(8,128)(2,1)} %param.8, f32[256,1024]{1,0:T(8,128)} %multiply_reduce_fusion, f32[256,1024]{1,0:T(8,128)} %copy-done.12), kind=kLoop, calls=%fused_computation.7 | loop fusion | flops 14155776 | bytes 17825792 | tf_op jit(solution)/shard_map/convert_element_type | solution.py:40
  759.8 3.4 copy.19
  (126 shorter events, 45.6 us)
Async XLA Ops:
  6.5 11.7 %copy-start = (bf16[1,6,256,1024]{3,2,1,0:T(8,128)(2,1)S(1)}, bf16[1,6,256,1024]{3,2,1,0:T(8,128)(2,1)}, u32[]{:S(2)}) copy-start(bf16[1,6,256,1024]{3,2,1,0:T(8,128)(2,1)} %param.9) | copy-start | bytes 9437188
  6.5 301.9 %all-gather.3.cloned.1.call-start = ((), (), s32[]{:S(2)}) async-start(), calls=%async_computation.1 | async-start | bytes 18874368 | tf_op jit(solution)/shard_map/all_gather | solution.py:93
  6.5 11.7 %copy-start.2 = (bf16[1,6,256,1024]{3,2,1,0:T(8,128)(2,1)S(1)}, bf16[1,6,256,1024]{3,2,1,0:T(8,128)(2,1)}, u32[]{:S(2)}) copy-start(bf16[1,6,256,1024]{3,2,1,0:T(8,128)(2,1)} %param.8) | copy-start | bytes 9437188
  17.3 1.0 copy-start.12
  68.2 5.4 copy-start.13
  77.9 0.8 copy-start.17
  77.9 1.6 copy-start.8
  79.5 1.6 copy-start.9
  338.3 1.6 copy-start.10
  339.9 4.6 copy-start.3
  342.1 4.3 collective-permute-start
  344.8 75.8 %copy-start.16 = (bf16[8,8,8,128]{3,2,1,0:T(8,128)(2,1)}, bf16[8,8,8,128]{3,2,1,0:T(8,128)(2,1)S(1)}, u32[]{:S(2)}) copy-start(bf16[8,8,8,128]{3,2,1,0:T(8,128)(2,1)S(1)} %copy.67) | copy-start | bytes 393220
  344.9 1.9 copy-start.11
  347.3 28.6 %slice-start = ((s8[16777216]{0:T(1024)(128)(4,1)}), s8[4194304]{0:T(1024)(128)(4,1)S(1)}, s32[]{:S(2)}) async-start(s8[16777216]{0:T(1024)(128)(4,1)} %bitcast.258), calls=%async_computation.3 | async-start | bytes 8388608
  347.3 28.6 %slice-start.1 = ((s8[16777216]{0:T(1024)(128)(4,1)}), s8[4194304]{0:T(1024)(128)(4,1)S(1)}, s32[]{:S(2)}) async-start(s8[16777216]{0:T(1024)(128)(4,1)} %bitcast.258), calls=%async_computation.4 | async-start | bytes 8388608
  347.3 28.6 %slice-start.2 = ((s8[16777216]{0:T(1024)(128)(4,1)}), s8[4194304]{0:T(1024)(128)(4,1)S(1)}, s32[]{:S(2)}) async-start(s8[16777216]{0:T(1024)(128)(4,1)} %bitcast.258), calls=%async_computation.5 | async-start | bytes 8388608
  358.1 17.3 %collective-permute-start.1 = (bf16[64,8192]{1,0:T(8,128)(2,1)S(1)}, bf16[64,8192]{1,0:T(8,128)(2,1)S(1)}, u32[]{:S(2)}, u32[]{:S(2)}) collective-permute-start(bf16[64,8192]{1,0:T(8,128)(2,1)S(1)} %fusion.17), channel_id=1, source_target_pairs={{0,8},{8,16},{16,24},{1,9},{9,17},{17,25},{2,10},{10,18},{18,26},{... | collective-permute-start | bytes 3145736 | tf_op jit(solution)/shard_map/ppermute | solution.py:16
  372.4 3.6 slice-start.3
  380.8 15.9 %collective-permute-start.2 = (bf16[64,8192]{1,0:T(8,128)(2,1)S(1)}, bf16[64,8192]{1,0:T(8,128)(2,1)S(1)}, u32[]{:S(2)}, u32[]{:S(2)}) collective-permute-start(bf16[64,8192]{1,0:T(8,128)(2,1)S(1)} %fusion.21), channel_id=1, source_target_pairs={{0,8},{8,16},{16,24},{1,9},{9,17},{17,25},{2,10},{10,18},{18,26},{... | collective-permute-start | bytes 3145736 | tf_op jit(solution)/shard_map/ppermute | solution.py:16
  402.1 16.4 %collective-permute-start.3 = (bf16[64,8192]{1,0:T(8,128)(2,1)S(1)}, bf16[64,8192]{1,0:T(8,128)(2,1)S(1)}, u32[]{:S(2)}, u32[]{:S(2)}) collective-permute-start(bf16[64,8192]{1,0:T(8,128)(2,1)S(1)} %fusion.25), channel_id=1, source_target_pairs={{0,8},{8,16},{16,24},{1,9},{9,17},{17,25},{2,10},{10,18},{18,26},{... | collective-permute-start | bytes 3145736 | tf_op jit(solution)/shard_map/ppermute | solution.py:16
  433.8 17.5 %copy-start.4 = (bf16[2,64,8192]{2,1,0:T(8,128)(2,1)S(1)}, bf16[2,64,8192]{2,1,0:T(8,128)(2,1)}, u32[]{:S(2)}) copy-start(bf16[2,64,8192]{2,1,0:T(8,128)(2,1)} %param.11) | copy-start | bytes 6291460
  436.4 14.9 %collective-permute-start.4 = (bf16[64,8192]{1,0:T(8,128)(2,1)S(1)}, bf16[64,8192]{1,0:T(8,128)(2,1)S(1)}, u32[]{:S(2)}, u32[]{:S(2)}) collective-permute-start(bf16[64,8192]{1,0:T(8,128)(2,1)S(1)} %fusion.30), channel_id=1, source_target_pairs={{8,0},{16,8},{24,16},{9,1},{17,9},{25,17},{10,2},{18,10},{26,18},{... | collective-permute-start | bytes 3145736 | tf_op jit(solution)/shard_map/ppermute | solution.py:16
  467.1 19.6 %copy-start.5 = (bf16[2,64,8192]{2,1,0:T(8,128)(2,1)S(1)}, bf16[2,64,8192]{2,1,0:T(8,128)(2,1)}, u32[]{:S(2)}) copy-start(bf16[2,64,8192]{2,1,0:T(8,128)(2,1)} %param.11) | copy-start | bytes 6291460
  469.8 16.9 %collective-permute-start.5 = (bf16[64,8192]{1,0:T(8,128)(2,1)S(1)}, bf16[64,8192]{1,0:T(8,128)(2,1)S(1)}, u32[]{:S(2)}, u32[]{:S(2)}) collective-permute-start(bf16[64,8192]{1,0:T(8,128)(2,1)S(1)} %fusion.11), channel_id=1, source_target_pairs={{8,0},{16,8},{24,16},{9,1},{17,9},{25,17},{10,2},{18,10},{26,18},{... | collective-permute-start | bytes 3145736 | tf_op jit(solution)/shard_map/ppermute | solution.py:16
  504.0 18.8 %copy-start.6 = (bf16[2,64,8192]{2,1,0:T(8,128)(2,1)S(1)}, bf16[2,64,8192]{2,1,0:T(8,128)(2,1)}, u32[]{:S(2)}) copy-start(bf16[2,64,8192]{2,1,0:T(8,128)(2,1)} %param.11) | copy-start | bytes 6291460
  506.7 16.1 %collective-permute-start.6 = (bf16[64,8192]{1,0:T(8,128)(2,1)S(1)}, bf16[64,8192]{1,0:T(8,128)(2,1)S(1)}, u32[]{:S(2)}, u32[]{:S(2)}) collective-permute-start(bf16[64,8192]{1,0:T(8,128)(2,1)S(1)} %fusion.12), channel_id=1, source_target_pairs={{8,0},{16,8},{24,16},{9,1},{17,9},{25,17},{10,2},{18,10},{26,18},{... | collective-permute-start | bytes 3145736 | tf_op jit(solution)/shard_map/ppermute | solution.py:16
  544.3 16.4 %collective-permute-start.7 = (bf16[64,8192]{1,0:T(8,128)(2,1)}, bf16[64,8192]{1,0:T(8,128)(2,1)}, u32[]{:S(2)}, u32[]{:S(2)}) collective-permute-start(bf16[64,8192]{1,0:T(8,128)(2,1)} %fusion.13), channel_id=1, source_target_pairs={{8,0},{16,8},{24,16},{9,1},{17,9},{25,17},{10,2},{18,10},{26,18},{... | collective-permute-start | bytes 3145736 | tf_op jit(solution)/shard_map/ppermute | solution.py:16
  552.6 4.8 copy-start.15
  552.6 8.2 %copy-start.7 = (bf16[2,64,8192]{2,1,0:T(8,128)(2,1)S(1)}, bf16[2,64,8192]{2,1,0:T(8,128)(2,1)}, u32[]{:S(2)}) copy-start(bf16[2,64,8192]{2,1,0:T(8,128)(2,1)} %param.11) | copy-start | bytes 6291460
  552.6 56.3 %all-to-all-start = ((bf16[128,8,1024]{0,2,1:T(8,128)(2,1)}), bf16[128,8,1024]{0,2,1:T(8,128)(2,1)}, u32[]{:S(2)}, u32[]{:S(2)}) async-start(bf16[128,8,1024]{0,2,1:T(8,128)(2,1)} %copy.14), calls=%async_computation | async-start | bytes 4194304 | tf_op jit(solution)/shard_map/all_to_all | solution.py:140
  557.0 85.2 %all-gather.5.cloned.1.call-start = ((), (), s32[]{:S(2)}) async-start(), calls=%async_computation.2 | async-start | bytes 2359296 | tf_op jit(solution)/shard_map/all_gather | solution.py:142
  562.5 0.7 copy-start.14
  681.6 20.9 %copy-start.1 = (bf16[1,6,256,1024]{3,2,1,0:T(8,128)(2,1)S(1)}, bf16[1,6,256,1024]{3,2,1,0:T(8,128)(2,1)}, u32[]{:S(2)}) copy-start(bf16[1,6,256,1024]{3,2,1,0:T(8,128)(2,1)} %param.9) | copy-start | bytes 9437188
Sparse Core Ops, SparseCore 0:
  78.1 230.3 all-gather.2
  563.4 78.8 all-gather.4
where the time goes:
time: 781 us; the launch traced here: 770 us
  waiting for transfers between devices  345 us (44%)
  other arithmetic  166 us (21%)
  local copies, waits for them, and re-layouts  105 us (13%)
  matrix products  87.4 us (11%)
  starting transfers between devices  53 us (7%)
  between operations  14.4 us (2%)
    all_gather x1, waiting for transfers between devices, per_device(): weights = lax.all_gather(masked, 'dp', axis=0, tiled=True)  224 us
    dot_general x4, matrix products, per_device(): lax.dot_general(vgrad, weights, (((1,), (1,)), ((), ())), preferred_eleme...  50.5 us
    ppermute x8, starting transfers between devices, shifted(): return lax.ppermute(x, axis, pairs)  48.5 us
    ppermute x8, waiting for transfers between devices, shifted(): return lax.ppermute(x, axis, pairs)  46.6 us
    another operation x2, local copies, waits for them, and re-layouts, mask_logit_backward(): jnp.stack([row_a + row_b, row_a + row_c, row_a + row_d, row_b + row_c, ro...  41.7 us
    all_to_all x1, waiting for transfers between devices, per_device(): lax.all_to_all(flat_u, 'dp', split_axis=1, concat_axis=0, tiled=True)  40.7 us
    all_gather x1, waiting for transfers between devices, per_device(): piece = lax.all_gather(flat_g, 'dp', axis=0, tiled=True)  33.4 us
    dot_general x4, matrix products, per_device(): value = jnp.dot(normed, weights, preferred_element_type=jnp.float32)  24.5 us
  transfers between devices with their start and end apart: 11, of which 7 were waited for; matrix products, arithmetic and copies ran while one was open for 4% of the time, Pallas kernels for 0%

commit v1 on v0

v1 whole, which is shorter than its diff:
```python
import jax
import jax.numpy as jnp
from jax import lax
from jax.sharding import PartitionSpec as P

VHEADS = 8


sharpness_divisor = 0.6666667
epsilon = 1e-05
F32 = jnp.float32
BF16 = jnp.bfloat16


def soft_mask(keeping_propensity, perturbed_draw):
    ranking_measure = (keeping_propensity.astype(F32) + perturbed_draw.astype(F32)) / sharpness_divisor
    expo = jnp.exp(ranking_measure)
    probs = expo / jnp.sum(expo, axis=0)
    first = probs[0] + probs[1] + probs[2]
    second = probs[0] + probs[3] + probs[4]
    third = probs[1] + probs[3] + probs[5]
    fourth = probs[2] + probs[4] + probs[5]
    mask = jnp.stack([first, second, third, fourth], axis=1)
    return (probs, mask.reshape(-1, mask.shape[-1]))


def mask_logit_backward(probs, weight, grads):
    dmask = (grads * weight.astype(F32)).reshape(-1, 4, grads.shape[-1])
    row_a, row_b, row_c, row_d = (dmask[:, 0], dmask[:, 1], dmask[:, 2], dmask[:, 3])
    dprob = jnp.stack([row_a + row_b, row_a + row_c, row_a + row_d, row_b + row_c, row_b + row_d, row_c + row_d])
    ranking_derivative = probs * (dprob - jnp.sum(probs * dprob, axis=0))
    return (ranking_derivative / sharpness_divisor).astype(BF16)


def collapse(x, kv_width):
    count, width = x.shape
    head = kv_width // VHEADS
    return jnp.sum(x.astype(F32).reshape(count, VHEADS, width // kv_width, head), axis=2).reshape(count, kv_width)


def dot(a, b, contract):
    return lax.dot_general(a, b, (contract, ((), ())), preferred_element_type=F32)


def per_device(value_weight, norm_gain, mask_logits, gumbel_noise, stream_in, stream_grad):
    section = lax.axis_index("section")
    sections = lax.axis_size("section")
    index, parts = lax.axis_index("dp"), lax.axis_size("dp")
    micro, rows, width = stream_in.shape
    weight = value_weight[0]
    block, kv = weight.shape
    head = kv // VHEADS
    repeat = width // kv
    local = min(block // head, repeat)
    heads = block // (local * head)
    sharers = parts * heads // VHEADS
    tokens = micro * rows
    x0 = stream_in.reshape(tokens, width)

    spread = lax.all_to_all(x0, "dp", split_axis=1, concat_axis=0, tiled=True)
    probs, mask = soft_mask(mask_logits[0], gumbel_noise[0])
    masked = (weight.astype(F32) * mask).astype(BF16)
    gain = lax.dynamic_slice_in_dim(norm_gain[0], index * block, block, 0).astype(F32)
    core = jnp.sum((masked.astype(F32) * gain[:, None]).reshape(heads, local, head, kv), axis=1).astype(BF16)
    cores = lax.all_gather(core.reshape(heads * head, kv), ("section", "dp"), axis=0, tiled=True)
    cores = cores.reshape(sections, VHEADS, sharers, head, kv)
    if sharers > 1:
        cores = jnp.sum(cores.astype(F32), axis=2).astype(BF16)
    cores = cores.reshape(sections, kv, kv)

    lhs = (spread.astype(F32) * gain).astype(BF16)
    part = dot(lhs, masked, ((1,), (0,))).astype(BF16)
    first = lax.psum_scatter(part, "dp", scatter_dimension=0, tiled=True)
    firsts = lax.all_gather(first, "section", axis=0, tiled=False).astype(F32)

    folded = collapse(x0, kv)
    square = jnp.sum(jnp.square(x0.astype(F32)), axis=1, keepdims=True)
    total = jnp.zeros((tokens, kv), F32)
    totals, scales, values = [], [], []
    for layer in range(sections):
        mean = square + 2 * jnp.sum(total * folded, axis=1, keepdims=True)
        mean = (mean + repeat * jnp.sum(total * total, axis=1, keepdims=True)) / width
        scale = lax.rsqrt(jnp.maximum(mean, 0) + epsilon)
        value = firsts[layer]
        if layer > 0:
            value = value + dot(total.astype(BF16), cores[layer], ((1,), (0,)))
        value = value * scale
        totals.append(total)
        scales.append(scale)
        values.append(value)
        total = total + value
    mine = lax.dynamic_index_in_dim(jnp.stack(totals), section, 0, keepdims=False).astype(BF16)
    mine = jnp.repeat(mine.reshape(tokens, parts // sharers, heads * head), sharers, axis=1)
    mine = mine.reshape(tokens, parts * heads * head)
    shift = lax.all_to_all(mine, "dp", split_axis=1, concat_axis=0, tiled=True)
    grad = collapse(stream_grad.reshape(tokens, width), kv)
    grads = [None] * sections
    for layer in range(sections - 1, -1, -1):
        vgrad = grad.astype(BF16)
        scale = scales[layer]
        grads[layer] = (vgrad.astype(F32) * scale).astype(BF16)
        if layer > 0:
            along = jnp.sum(vgrad.astype(F32) * values[layer], axis=1, keepdims=True) / width
            grad = grad + scale * dot(vgrad, cores[layer], ((1,), (1,)))
            grad = grad - scale * scale * along * (folded + repeat * totals[layer])
    sent = lax.dynamic_index_in_dim(jnp.stack(grads), section, 0, keepdims=False)
    right = lax.all_gather(sent, "dp", axis=0, tiled=True)

    count = right.shape[0]
    grown = jnp.broadcast_to(shift.reshape(count, heads, 1, head), (count, heads, local, head)).reshape(count, block)
    left = (spread.astype(F32) + grown.astype(F32)).astype(BF16)
    wgrad = dot(left, right, ((0,), (0,))) * gain[:, None]
    return mask_logit_backward(probs, weight, wgrad)[None]


def solution(mesh):
    return jax.shard_map(
        per_device,
        mesh=mesh,
        in_specs=(
            P("section", "dp", None),
            P("section", None),
            P("section", None, "dp", None),
            P("section", None, "dp", None),
            P(None, "dp", None),
            P(None, "dp", None),
        ),
        out_specs=P("section", None, "dp", None),
        check_vma=False,
    )
```

time: 781 us -> 357 us (0.46)
  waiting for transfers between devices: 345 us -> 171 us
  other arithmetic: 166 us -> 61.9 us
  matrix products: 87.4 us -> 22.1 us
  local copies, waits for them, and re-layouts: 105 us -> 57.7 us
  starting transfers between devices: 53 us -> 8.14 us
  blocking collectives: 0 us -> 19 us
    all_gather x2 -> x3, waiting for transfers between devices: 257 us -> 82.2 us  [the longest x1 55.4 us: per_device(): lax.all_gather(core.reshape(heads * head, kv), ('section', 'dp'), axis=0,...]
    reduce_scatter x0 -> x1, waiting for transfers between devices: none -> 67.5 us  [per_device(): first = lax.psum_scatter(part, 'dp', scatter_dimension=0, tiled=True)]
    dot_general x9 -> x8, matrix products: 87.4 us -> 22.1 us  [dot(): lax.dot_general(a, b, (contract, ((), ())), preferred_element_type=F32)]
    ppermute x8 -> x0, starting transfers between devices: 48.5 us -> none  [shifted(): return lax.ppermute(x, axis, pairs)]
    ppermute x8 -> x0, waiting for transfers between devices: 46.6 us -> none  [shifted(): return lax.ppermute(x, axis, pairs)]
    another operation x4 -> x2, local copies, waits for them, and re-layouts: 43.5 us -> 4.68 us  [the longest x1 4.67 us: soft_mask(): mask = jnp.stack([first, second, third, fourth], axis=1)]
    add x1, other arithmetic: 23.8 us -> 0.93 us  [soft_mask(): first = probs[0] + probs[1] + probs[2]]
    dot_general x2 -> x0, local copies, waits for them, and re-layouts: 20.9 us -> none  [per_device(): value = jnp.dot(normed, weights, preferred_element_type=jnp.float32)]
  transfers between devices with their start and end apart: 11 -> 5, of which waited for: 7 -> 4; matrix products, arithmetic and copies ran while one was open for 4% -> 19% of each run, Pallas kernels for 0% -> 0%
where the time goes in v1:
time: 357 us; the launch traced here: 353 us
  waiting for transfers between devices  171 us (48%)
  other arithmetic  61.9 us (17%)
  local copies, waits for them, and re-layouts  57.7 us (16%)
  matrix products  22.1 us (6%)
  blocking collectives  19 us (5%)
  between operations  13.8 us (4%)
  starting transfers between devices  8.14 us (2%)
    reduce_scatter x1, waiting for transfers between devices, per_device(): first = lax.psum_scatter(part, 'dp', scatter_dimension=0, tiled=True)  67.5 us
    all_gather x1, waiting for transfers between devices, per_device(): lax.all_gather(core.reshape(heads * head, kv), ('section', 'dp'), axis=0,...  55.4 us
    all_gather x1, waiting for transfers between devices, per_device(): right = lax.all_gather(sent, 'dp', axis=0, tiled=True)  26.7 us
    dot_general x8, matrix products, dot(): lax.dot_general(a, b, (contract, ((), ())), preferred_element_type=F32)  22.1 us
    all_to_all x1, waiting for transfers between devices, per_device(): spread = lax.all_to_all(x0, 'dp', split_axis=1, concat_axis=0, tiled=True)  21.1 us
    all_to_all x1, blocking collectives, per_device(): shift = lax.all_to_all(mine, 'dp', split_axis=1, concat_axis=0, tiled=True)  19 us
    unnamed x14, other arithmetic  16.3 us
    unnamed x44, local copies, waits for them, and re-layouts  12.4 us
  transfers between devices with their start and end apart: 5, of which 4 were waited for; matrix products, arithmetic and copies ran while one was open for 19% of the time, Pallas kernels for 0%

profile of v1, /device:TPU:0, one launch (start us, length us, event | category | flops | bytes accessed | tf_op | source)
XLA Modules:
  0.0 353.5 jit_solution(6608914108023606095)
XLA Ops:
  6.5 3.0 copy.43
  9.5 2.5 copy.30
  12.0 7.3 %all-to-all-start = ((bf16[128,8,1024]{2,0,1:T(8,128)(2,1)}), bf16[128,8,1024]{2,0,1:T(8,128)(2,1)}, u32[]{:S(2)}, u32[]{:S(2)}) async-start(bf16[128,8,1024]{2,0,1:T(8,128)(2,1)} %copy.30), calls=%async_computation | async-start | bytes 4194304 | tf_op jit(solution)/shard_map/all_to_all | solution.py:60
  19.9 5.0 %reshape.690 = f32[256,4,1024]{2,1,0:T(4,128)} reshape(bf16[1,1024,1024]{2,1,0:T(8,128)(2,1)} %param.6) | data formatting | bytes 6291456 | tf_op jit(solution)/shard_map/convert_element_type | solution.py:62
  24.9 3.8 %fusion.2 = f32[256,1024]{1,0:T(8,128)S(1)} fusion(bf16[1,6,256,1024]{3,2,1,0:T(8,128)(2,1)S(1)} %copy-done.1, bf16[1,6,256,1024]{3,2,1,0:T(8,128)(2,1)} %param.8), kind=kLoop, calls=%fused_computation.14 | loop fusion | flops 7602176 | bytes 7340032 | tf_op jit(solution)/shard_map/reduce_sum | solution.py:18
  28.7 1.6 bitcast_divide_fusion
  31.3 2.2 copy-done
  33.5 1.3 copy-done.6
  34.8 4.1 %fusion.1 = (bf16[256,4,1024]{2,0,1:T(8,128)(2,1)S(1)}, f32[256,4,1024]{2,0,1:T(8,128)}) fusion(f32[256,4,1024]{2,1,0:T(4,128)S(1)} %copy-done.6, f32[256,1,1024]{2,0,1:T(8,128)S(1)} %get-tuple-element.15, f32[256,1,1024]{2,0,1:T(8,128)S(1)} %get-tuple-element.16, f32[256,1,1024]{2,0,1:T(8,128)S(1)} %get-tuple-element.14, ...), kind=kLoop, calls=%fused_computation.9 | loop fusion | flops 5242880 | bytes 14680064 | tf_op jit(solution)/shard_map/convert_element_type | solution.py:62
  38.9 2.9 copy.32
  41.9 4.0 %convert_element_type.254 = bf16[1024,1024]{1,0:T(8,128)(2,1)} reshape(bf16[256,4,1024]{2,1,0:T(4,128)(2,1)} %copy.32) | data formatting | bytes 4194304 | tf_op jit(solution)/shard_map/convert_element_type | solution.py:62
  46.6 21.1 %all-to-all-done = bf16[128,8,1024]{2,0,1:T(8,128)(2,1)} async-done(((bf16[128,8,1024]{2,0,1:T(8,128)(2,1)}), bf16[128,8,1024]{2,0,1:T(8,128)(2,1)}, u32[]{:S(2)}, u32[]{:S(2)}) %all-to-all-start) | async-done | bytes 2097184 | tf_op jit(solution)/shard_map/all_to_all | solution.py:60
  67.6 2.3 multiply_convert_fusion.2
  69.9 3.7 %convolution_convert_fusion = bf16[1024,1024]{1,0:T(8,128)(2,1)} fusion(bf16[1024,1024]{1,0:T(8,128)(2,1)S(1)} %bitcast.141, bf16[1024,1024]{1,0:T(8,128)(2,1)S(1)} %copy-done.16), kind=kOutput, calls=%fused_computation.19 | convolution fusion | flops 2148532224 | bytes 6291456 | tf_op jit(solution)/shard_map/dot_general | solution.py:42
  73.7 67.5 %reduce-scatter.2.cloned.1.call-done = bf16[128,1024]{1,0:T(8,128)(2,1)} async-done(((bf16[1024,1024]{1,0:T(8,128)(2,1)}), bf16[128,1024]{1,0:T(8,128)(2,1)}) %reduce-scatter.2.cloned.1.call-update) | async-done | bytes 262160 | tf_op jit(solution)/shard_map/reduce_scatter | solution.py:73
  141.4 4.2 %convert_element_type.298 = f32[1,1024,1024]{2,1,0:T(8,128)} convert(bf16[1,1024,1024]{2,1,0:T(8,128)(2,1)} %param.6) | non-fusion elementwise | flops 1048576 | bytes 6291456 | tf_op jit(solution)/shard_map/convert_element_type | solution.py:62
  145.6 4.7 %copy.33 = f32[256,4,1024]{2,1,0:T(4,128)} copy(f32[256,4,1024]{2,0,1:T(8,128)S(1)} %copy-done.5) | data formatting | bytes 8388608 | tf_op jit(solution)/shard_map/stack | solution.py:23
  150.3 5.3 %reshape.684 = f32[1,8,128,1024]{3,2,1,0:T(8,128)} reshape(f32[256,4,1024]{2,1,0:T(4,128)} %copy.33) | data formatting | bytes 8388608 | tf_op jit(solution)/shard_map/reshape | solution.py:24
  155.6 4.7 %multiply_reduce_fusion.1 = bf16[128,1024]{1,0:T(8,128)(2,1)} fusion(f32[1,8,128,1024]{3,2,1,0:T(8,128)} %bitcast.136, f32[1,8,128,1024]{3,2,1,0:T(8,128)} %reshape.684, f32[8,128]{1,0:T(8,128)S(1)} %bitcast.146), kind=kLoop, calls=%fused_computation.10 | loop fusion | flops 5111808 | bytes 8654848 | tf_op jit(solution)/shard_map/reduce_sum | solution.py:64
  160.4 3.0 reduce.6
  163.4 2.0 copy.124
  165.3 2.1 multiply_reduce_fusion.2
  167.5 1.9 reduce_sum.158
  169.4 3.0 reduce.7
  172.5 1.1 copy.125
  175.2 1.9 reshape.696
  177.2 2.1 multiply_reduce_fusion.7
  179.3 1.5 convert_element_type.308
  180.9 1.1 copy-done.9
  182.1 1.2 multiply_reduce_fusion.6
  183.3 55.4 %all-gather.6.cloned.1.call-done = bf16[4096,1024]{1,0:T(8,128)(2,1)} async-done(((bf16[128,1024]{1,0:T(8,128)(2,1)}), bf16[4096,1024]{1,0:T(8,128)(2,1)}) %all-gather.6.cloned.1.call-update) | async-done | bytes 8388624 | tf_op jit(solution)/shard_map/all_gather | solution.py:65
  238.7 3.0 fusion.90
  241.8 2.5 fusion.91
  244.5 3.0 fusion.76
  253.1 19.0 %all_to_all.23 = bf16[128,8,128]{2,0,1:T(8,128)(2,1)S(1)} all-to-all(bf16[128,8,128]{2,0,1:T(8,128)(2,1)S(1)} %copy.34), channel_id=1, replica_groups=mesh['section'=4,'dp'=8] {'dp'}, dimensions={1} | all-to-all | bytes 524288 | tf_op jit(solution)/shard_map/all_to_all | solution.py:95
  272.4 4.1 %fusion = bf16[1024,1024]{1,0:T(8,128)(2,1)} fusion(f32[128,8,8,128]{3,2,1,0:T(8,128)S(1)} %bitcast.137, bf16[128,8,1024]{2,0,1:T(8,128)(2,1)} %all-to-all-done), kind=kLoop, calls=%fused_computation.5 | loop fusion | flops 3145728 | bytes 8388608 | tf_op jit(solution)/shard_map/convert_element_type | solution.py:111
  276.5 26.7 %all-gather.10.cloned.1.call-done = bf16[1,1024,1024]{2,1,0:T(8,128)(2,1)} async-done(((bf16[1,128,1024]{2,1,0:T(8,128)(2,1)}), bf16[1,1024,1024]{2,1,0:T(8,128)(2,1)}) %all-gather.10.cloned.1.call-update) | async-done | bytes 2097168 | tf_op jit(solution)/shard_map/all_gather | solution.py:107
  303.2 7.2 %bitcast_multiply_fusion = f32[1024,1024]{1,0:T(8,128)} fusion(bf16[1024,1024]{1,0:T(8,128)(2,1)} %fusion, bf16[1,1024,1024]{2,1,0:T(8,128)(2,1)} %all-gather.10.cloned.1.call-done, f32[1024]{0:T(1024)S(1)} %bitcast.147, bf16[1,1024,1024]{2,1,0:T(8,128)(2,1)} %param.6), kind=kOutput, calls=%fused_computation.7 | convolution fusion | flops 2150629376 | bytes 10489856 | tf_op jit(solution)/shard_map/dot_general | solution.py:42
  310.4 5.2 %reshape.687 = f32[256,4,1024]{2,1,0:T(4,128)} reshape(f32[1024,1024]{1,0:T(8,128)} %bitcast_multiply_fusion) | data formatting | bytes 8388608 | tf_op jit(solution)/shard_map/reshape | solution.py:28
  315.6 10.9 %fusion.110 = (f32[256,1,1024]{2,1,0:T(1,128)S(1)}, f32[256,1,1024]{2,1,0:T(1,128)S(1)}, f32[256,1,1024]{2,1,0:T(1,128)S(1)}, f32[256,1,1024]{2,1,0:T(1,128)S(1)}) fusion(f32[256,4,1024]{2,1,0:T(4,128)} %reshape.687), kind=kLoop, calls=%fused_computation.133 | loop fusion | bytes 8388608 | tf_op jit(solution)/shard_map/slice | solution.py:29
  326.5 1.4 bitcast_dynamic-update-slice_fusion.5
  328.3 1.5 bitcast_dynamic-update-slice_fusion.4
  329.8 1.4 bitcast_dynamic-update-slice_fusion.3
  331.2 1.4 bitcast_dynamic-update-slice_fusion.2
  332.7 1.4 bitcast_dynamic-update-slice_fusion.1
  334.1 1.5 bitcast_dynamic-update-slice_fusion
  335.6 4.4 %multiply_reduce_fusion = f32[256,1024]{1,0:T(8,128)S(1)} fusion(f32[6,256,1024]{2,1,0:T(8,128)S(1)} %bitcast.132, f32[6,256,1024]{2,1,0:T(8,128)} %bitcast_dynamic-update-slice_fusion), kind=kLoop, calls=%fused_computation.2 | loop fusion | flops 2883584 | bytes 13631488 | tf_op jit(solution)/shard_map/reduce_sum | solution.py:31
  343.1 3.6 %multiply_convert_fusion = bf16[1,6,256,1024]{3,2,1,0:T(8,128)(2,1)} fusion(f32[1,6,256,1024]{3,2,1,0:T(8,128)S(1)} %bitcast_dynamic-update-slice_fusion.6, bf16[1,6,256,1024]{3,2,1,0:T(8,128)(2,1)S(1)} %copy-done.1, bf16[1,6,256,1024]{3,2,1,0:T(8,128)(2,1)S(1)} %copy-done.3, f32[256,1024]{1,0:T(8,128)S(1)} %multiply_reduce_fusion, f32[256,1024]{1,0:T(8,128)S(1)} %copy-done.8), kind=kLoop, calls=%fused_computation.1 | loop fusion | flops 14155776 | bytes 17825792 | tf_op jit(solution)/shard_map/convert_element_type | solution.py:32
  (79 shorter events, 14.0 us)
Async XLA Ops:
  12.0 55.6 %all-to-all-start = ((bf16[128,8,1024]{2,0,1:T(8,128)(2,1)}), bf16[128,8,1024]{2,0,1:T(8,128)(2,1)}, u32[]{:S(2)}, u32[]{:S(2)}) async-start(bf16[128,8,1024]{2,0,1:T(8,128)(2,1)} %copy.30), calls=%async_computation | async-start | bytes 4194304 | tf_op jit(solution)/shard_map/all_to_all | solution.py:60
  19.3 5.6 %copy-start.1 = (bf16[1,6,256,1024]{3,2,1,0:T(8,128)(2,1)S(1)}, bf16[1,6,256,1024]{3,2,1,0:T(8,128)(2,1)}, u32[]{:S(2)}) copy-start(bf16[1,6,256,1024]{3,2,1,0:T(8,128)(2,1)} %param.9) | copy-start | bytes 9437188
  19.3 121.9 %reduce-scatter.2.cloned.1.call-start = ((), (), s32[]{:S(2)}) async-start(), calls=%async_computation.3 | async-start | bytes 2359296 | tf_op jit(solution)/shard_map/reduce_scatter | solution.py:73
  24.9 3.8 %copy-start.2 = (bf16[1,6,256,1024]{3,2,1,0:T(8,128)(2,1)S(1)}, bf16[1,6,256,1024]{3,2,1,0:T(8,128)(2,1)}, u32[]{:S(2)}) copy-start(bf16[1,6,256,1024]{3,2,1,0:T(8,128)(2,1)} %param.8) | copy-start | bytes 9437188
  28.7 1.6 copy-start.7
  30.3 3.2 copy-start
  30.3 4.5 %copy-start.6 = (f32[256,4,1024]{2,1,0:T(4,128)S(1)}, f32[256,4,1024]{2,1,0:T(4,128)}, u32[]{:S(2)}) copy-start(f32[256,4,1024]{2,1,0:T(4,128)} %reshape.690) | copy-start | bytes 12582916
  67.6 2.3 copy-start.16
  73.6 105.6 %all-gather.8.cloned.1.call-start = ((), (), s32[]{:S(2)}) async-start(), calls=%async_computation.5 | async-start | bytes 1310720 | tf_op jit(solution)/shard_map/all_gather | solution.py:74
  141.2 97.5 %all-gather.6.cloned.1.call-start = ((), (), s32[]{:S(2)}) async-start(), calls=%async_computation.4 | async-start | bytes 8650752 | tf_op jit(solution)/shard_map/all_gather | solution.py:65
  141.4 4.2 %copy-start.5 = (f32[256,4,1024]{2,0,1:T(8,128)S(1)}, f32[256,4,1024]{2,0,1:T(8,128)}, u32[]{:S(2)}) copy-start(f32[256,4,1024]{2,0,1:T(8,128)} %get-tuple-element.22) | copy-start | bytes 12582916
  160.3 142.9 %all-gather.10.cloned.1.call-start = ((), (), s32[]{:S(2)}) async-start(), calls=%async_computation.6 | async-start | bytes 2359296 | tf_op jit(solution)/shard_map/all_gather | solution.py:107
  173.6 0.8 copy-start.12
  180.7 1.3 copy-start.9
  238.7 3.1 copy-start.4
  238.7 3.1 copy-start.10
  238.7 5.6 %copy-start.17 = (f32[1,128,1024]{2,1,0:T(8,128)S(1)}, f32[1,128,1024]{2,1,0:T(8,128)}, u32[]{:S(2)}) copy-start(f32[1,128,1024]{2,1,0:T(8,128)} %reshape.696) | copy-start | bytes 1572868
  238.7 5.7 %copy-start.13 = (f32[16,8,8,128]{3,2,1,0:T(8,128)S(1)}, f32[16,8,8,128]{3,2,1,0:T(8,128)}, u32[]{:S(2)}) copy-start(f32[16,8,8,128]{3,2,1,0:T(8,128)} %copy-done.12) | copy-start | bytes 1572868
  241.8 6.8 %copy-start.14 = (f32[128,1024]{1,0:T(8,128)}, f32[128,1024]{1,0:T(8,128)S(1)}, u32[]{:S(2)}) copy-start(f32[128,1024]{1,0:T(8,128)S(1)} %get-tuple-element.10) | copy-start | bytes 1572868
  241.8 5.6 %copy-start.11 = (bf16[4096,1024]{1,0:T(8,128)(2,1)S(1)}, bf16[4096,1024]{1,0:T(8,128)(2,1)}, u32[]{:S(2)}) copy-start(bf16[4096,1024]{1,0:T(8,128)(2,1)} %all-gather.6.cloned.1.call-done) | copy-start | bytes 25165828
  244.3 4.1 %copy-start.15 = (f32[128,1024]{1,0:T(8,128)}, f32[128,1024]{1,0:T(8,128)S(1)}, u32[]{:S(2)}) copy-start(f32[128,1024]{1,0:T(8,128)S(1)} %get-tuple-element.9) | copy-start | bytes 1572868
  329.8 5.7 %slice-start = ((s8[6291456]{0:T(1024)(128)(4,1)}), s8[4194304]{0:T(1024)(128)(4,1)S(1)}, s32[]{:S(2)}) async-start(s8[6291456]{0:T(1024)(128)(4,1)} %bitcast.131), calls=%async_computation.7 | async-start | bytes 8388608
  331.2 4.3 %slice-start.1 = ((s8[6291456]{0:T(1024)(128)(4,1)}), s8[2097152]{0:T(1024)(128)(4,1)S(1)}, s32[]{:S(2)}) async-start(s8[6291456]{0:T(1024)(128)(4,1)} %bitcast.131), calls=%async_computation.8 | async-start | bytes 4194304
  340.9 1.9 copy-start.3
  340.9 2.2 copy-start.8
Sparse Core Ops, SparseCore 0:
  73.7 67.3 reduce-scatter.1
  142.7 15.6 all-gather.7
  161.4 77.2 all-gather.5
  251.6 51.5 all-gather.9

commit v2 on v1

v2 whole, which is shorter than its diff:
```python
import functools

import jax
import jax.numpy as jnp
from jax import lax
from jax.experimental import pallas as pl
from jax.experimental.pallas import tpu as pltpu
from jax.sharding import PartitionSpec as P

VHEADS = 8


sharpness_divisor = 0.6666667
epsilon = 1e-05
F32 = jnp.float32
BF16 = jnp.bfloat16
MESH = pl.DeviceIdType.MESH
LIMIT = 60 * 1024 * 1024


def dot(a, b, contract):
    return lax.dot_general(a, b, (contract, ((), ())), preferred_element_type=F32)


def planar(size):
    feature = lax.broadcasted_iota(jnp.int32, (size, size), 0)
    position = lax.broadcasted_iota(jnp.int32, (size, size), 1)
    groups = size // 4
    return (feature == 4 * (position % groups) + position // groups).astype(F32).astype(BF16)


def pattern_probs(logits_ref, noise_ref):
    scores = [
        jnp.exp((logits_ref[k].astype(F32) + noise_ref[k].astype(F32)) / sharpness_divisor) for k in range(6)
    ]
    inverse = 1.0 / (scores[0] + scores[1] + scores[2] + scores[3] + scores[4] + scores[5])
    return [score * inverse for score in scores]


def mask_kernel(local, head, logits_ref, noise_ref, weight_ref, gain_ref, masked_ref, core_ref, total):
    size = weight_ref.shape[0]
    groups = size // 4
    order = planar(size)
    p = pattern_probs(logits_ref, noise_ref)
    planes = [p[0] + p[1] + p[2], p[0] + p[3] + p[4], p[1] + p[3] + p[5], p[2] + p[4] + p[5]]
    apart = dot(order, weight_ref[...], ((0,), (0,)))
    rows = [(apart[r * groups:(r + 1) * groups] * planes[r]).astype(BF16) for r in range(4)]
    masked = dot(order, jnp.concatenate(rows, axis=0), ((1,), (0,)))
    masked_ref[...] = masked.astype(BF16)
    term = masked * gain_ref[...]

    @pl.when(pl.program_id(0) % local == 0)
    def _():
        total[...] = term

    @pl.when(pl.program_id(0) % local != 0)
    def _():
        total[...] += term

    core_ref[...] = total[...].astype(BF16)


def logit_kernel(logits_ref, noise_ref, weight_ref, gain_ref, spread_ref, shift_ref, right_ref, out_ref):
    size = weight_ref.shape[0]
    groups = size // 4
    order = planar(size)
    left = (spread_ref[...].astype(F32) + shift_ref[...].astype(F32)) * gain_ref[...]
    left = dot(left.astype(BF16), order, ((1,), (0,))).astype(BF16)
    wgrad = dot(left, right_ref[...], ((0,), (0,)))
    grad = wgrad * dot(order, weight_ref[...], ((0,), (0,)))
    a, b, c, d = [grad[r * groups:(r + 1) * groups] for r in range(4)]
    p = pattern_probs(logits_ref, noise_ref)
    dprob = [a + b, a + c, a + d, b + c, b + d, c + d]
    mean = sum(p[k] * dprob[k] for k in range(6))
    for k in range(6):
        out_ref[k] = (p[k] * (dprob[k] - mean) / sharpness_divisor).astype(BF16)


def relay_kernel(
    n, sections, sharers, x0_ref, top_ref, gain_ref, masked_ref, core_ref, spread_ref, shift_ref, right_ref,
    cores, parts, fromy, fromz, sums, full, hop, mine,
    a_send, a_recv, b_send, b_recv, c_send, c_recv, d_send, y_send, y_recv, z_send, z_recv,
    h_send, h_recv, v_send, v_recv, g_send, g_recv, f_send, own_sem,
):
    me, sec = lax.axis_index("dp"), lax.axis_index("section")
    half_n = n // 2
    lane = me % 2
    mate = me + 1 - 2 * lane
    twin = sec + 1 - 2 * (sec % 2)
    tokens, width = x0_ref.shape
    block = spread_ref.shape[2]
    kv = masked_ref.shape[1]
    head = kv // VHEADS
    repeat = width // kv
    half = tokens // 2

    def at(k):
        return lax.rem(me + k + n, n)

    barrier = pltpu.get_barrier_semaphore()

    @pl.loop(1, n)
    def _(k):
        pl.semaphore_signal(barrier, inc=1, device_id=(sec, at(k)), device_id_type=MESH)

    for step in (1, sections - 1):
        pl.semaphore_signal(barrier, inc=1, device_id=(lax.rem(sec + step, sections), me), device_id_type=MESH)
    pl.semaphore_wait(barrier, n + 1)

    def copy(src, dst, send, recv, where):
        return pltpu.make_async_remote_copy(
            src_ref=src, dst_ref=dst, send_sem=send, recv_sem=recv, device_id=where, device_id_type=MESH
        )

    rows = pl.ds(pl.multiple_of((sec % 2) * half, half), half)
    others = pl.ds(pl.multiple_of((1 - sec % 2) * half, half), half)

    def spread_out(k):
        dest = at(k)
        cols = pl.ds(pl.multiple_of(dest * block, block), block)
        return copy(x0_ref.at[rows, cols], spread_ref.at[me, rows], a_send.at[k], a_recv.at[me], (sec, dest))

    def spread_in(src):
        return copy(spread_ref.at[src, rows], spread_ref.at[src, rows], a_send.at[0], a_recv.at[src], (sec, mate))

    def twin_out(src):
        return copy(spread_ref.at[src, rows], spread_ref.at[src, rows], b_send.at[src], b_recv.at[src], (twin, me))

    def twin_in(src):
        return copy(spread_ref.at[src, others], spread_ref.at[src, others], b_send.at[src], b_recv.at[src], (twin, me))

    own_cols = pl.ds(pl.multiple_of(me * block, block), block)
    own = pltpu.make_async_copy(x0_ref.at[:, own_cols], spread_ref.at[me], own_sem)
    own.start()

    @pl.loop(1, n)
    def _(k):
        spread_out(k).start()

    def gather_out(buf, send, recv, k):
        return copy(buf.at[me], buf.at[me], send.at[k], recv.at[me], (sec, at(2 * k)))

    def gather_pass(buf, send, recv, k):
        src = at(-2 * k)
        return copy(buf.at[src], buf.at[src], send.at[k], recv.at[src], (sec, mate))

    def gather_in(buf, send, recv, src):
        return copy(buf.at[src], buf.at[src], send.at[0], recv.at[src], (sec, mate))

    def gather_start(buf, send, more, recv):
        gather_pass(buf, more, recv, 0).start()

        @pl.loop(1, half_n)
        def _(k):
            gather_out(buf, send, recv, k).start()

    def gather_forward(buf, send, more, recv, k):
        gather_in(buf, send, recv, at(-2 * k)).wait_recv()
        gather_pass(buf, more, recv, k).start()

    def gather_end(buf, send, more, recv):
        @pl.loop(0, half_n)
        def _(k):
            pair = at(-2 * k)
            gather_in(buf, send, recv, pair + 1 - 2 * lane).wait_recv()
            gather_pass(buf, more, recv, k).wait_send()

        @pl.loop(1, half_n)
        def _(k):
            gather_out(buf, send, recv, k).wait_send()

    cores[me] = core_ref[...]
    gather_start(cores, c_send, d_send, c_recv)

    def product(src):
        lhs = (spread_ref[src].astype(F32) * gain_ref[...]).astype(BF16)
        parts[src] = dot(lhs, masked_ref[...], ((1,), (0,))).astype(BF16)

    def mate_out(owner):
        return copy(parts.at[owner], fromy.at[owner // 2], y_send.at[owner // 2], y_recv.at[owner // 2], (sec, mate))

    def mate_in(owner):
        return copy(parts.at[owner], fromy.at[owner // 2], y_send.at[owner // 2], y_recv.at[owner // 2], (sec, mate))

    def arrive(k):
        src = at(-k)
        spread_in(src).wait_recv()
        twin_out(src).start()

    def whole(k):
        src = at(-k)
        twin_in(src).wait_recv()
        product(src)

    arrive(1)

    @pl.loop(1, half_n)
    def _(j):
        arrive(2 * j)
        whole(2 * j - 1)
        mate_out(at(1 - 2 * j)).start()
        arrive(2 * j + 1)
        whole(2 * j)
        gather_forward(cores, c_send, d_send, c_recv, j)

    whole(n - 1)
    mate_out(at(1 - n)).start()
    own.wait()
    product(me)

    folded = []
    tops = []
    square = jnp.zeros((tokens, 1), F32)
    for h in range(VHEADS):
        low = jnp.zeros((tokens, head), F32)
        high = jnp.zeros((tokens, head), F32)
        power = jnp.zeros((tokens, head), F32)
        for r in range(repeat):
            cols = slice((h * repeat + r) * head, (h * repeat + r + 1) * head)
            x = x0_ref[:, cols].astype(F32)
            low = low + x
            power = power + x * x
            high = high + top_ref[:, cols].astype(F32)
        folded.append(low)
        tops.append(high)
        square = square + jnp.sum(power, axis=1, keepdims=True)
    sums[...] = jnp.concatenate(folded, axis=1)
    hop[0] = jnp.concatenate(tops, axis=1).astype(BF16)

    def lane_out(k):
        owner = at(2 * k)
        return copy(parts.at[owner], fromz.at[me // 2], z_send.at[k], z_recv.at[me // 2], (sec, owner))

    def lane_in(src):
        return copy(parts.at[src], fromz.at[src // 2], z_send.at[0], z_recv.at[src // 2], (sec, mate))

    @pl.loop(1, half_n)
    def _(j):
        k = half_n - j
        owner = at(2 * k)
        mate_in(owner).wait_recv()
        parts[owner] = (parts[owner].astype(F32) + fromy[owner // 2].astype(F32)).astype(BF16)
        lane_out(k).start()

    mate_in(me).wait_recv()
    full[...] = parts[me].astype(F32) + fromy[me // 2].astype(F32)

    @pl.loop(1, half_n)
    def _(k):
        src = at(-2 * k)
        lane_in(src).wait_recv()
        full[...] += fromz[src // 2].astype(F32)

    gather_end(cores, c_send, d_send, c_recv)

    def core():
        if sharers == 1:
            return cores[...].reshape(kv, kv)
        group = cores[...].astype(F32).reshape(kv // cores.shape[1], sharers, cores.shape[1], kv)
        return jnp.sum(group, axis=1).astype(BF16).reshape(kv, kv)

    up = lax.rem(sec + 1, sections)
    down = lax.rem(sec + sections - 1, sections)

    @pl.when(sec == 0)
    def _():
        hop[2] = jnp.zeros((tokens, kv), BF16)

    @pl.when(sec > 0)
    def _():
        copy(mine, hop.at[2], h_send.at[0], h_recv.at[0], (down, me)).wait_recv()

    total = hop[2].astype(F32)
    mean = square + 2 * jnp.sum(total * sums[...], axis=1, keepdims=True)
    mean = (mean + repeat * jnp.sum(total * total, axis=1, keepdims=True)) / width
    scale = lax.rsqrt(jnp.maximum(mean, 0) + epsilon)
    full[...] = (full[...] + dot(hop[2], core(), ((1,), (0,)))) * scale
    mine[...] = (total + full[...]).astype(BF16)

    @pl.when(sec < sections - 1)
    def _():
        copy(mine, hop.at[2], h_send.at[0], h_recv.at[0], (up, me)).start()

    share = shift_ref.shape[2]

    def share_of(dest):
        return pl.ds(pl.multiple_of((dest // sharers) * share, share), share)

    def shift_out(k):
        dest = at(k)
        return copy(hop.at[2, :, share_of(dest)], shift_ref.at[me], v_send.at[k], v_recv.at[me], (sec, dest))

    @pl.loop(1, n)
    def _(k):
        shift_out(k).start()

    local = pltpu.make_async_copy(hop.at[2, :, share_of(me)], shift_ref.at[me], own_sem)
    local.start()

    @pl.when(sec == sections - 1)
    def _():
        hop[1] = hop[0]

    @pl.when(sec < sections - 1)
    def _():
        copy(hop.at[3], hop.at[1], h_send.at[1], h_recv.at[1], (up, me)).wait_recv()

    vgrad = hop[1].astype(F32)

    @pl.when(sec > 0)
    def _():
        along = jnp.sum(vgrad * full[...], axis=1, keepdims=True) / width
        below = vgrad + scale * dot(hop[1], core(), ((1,), (1,)))
        below = below - scale * scale * along * (sums[...] + repeat * hop[2].astype(F32))
        hop[3] = below.astype(BF16)
        copy(hop.at[3], hop.at[1], h_send.at[1], h_recv.at[1], (down, me)).start()

    right_ref[me] = (vgrad * scale).astype(BF16)
    gather_start(right_ref, g_send, f_send, g_recv)

    @pl.loop(1, half_n)
    def _(k):
        gather_forward(right_ref, g_send, f_send, g_recv, k)

    gather_end(right_ref, g_send, f_send, g_recv)
    local.wait()

    @pl.when(sec < sections - 1)
    def _():
        copy(mine, hop.at[2], h_send.at[0], h_recv.at[0], (up, me)).wait_send()

    @pl.when(sec > 0)
    def _():
        copy(hop.at[3], hop.at[1], h_send.at[1], h_recv.at[1], (down, me)).wait_send()

    @pl.loop(1, n)
    def _(k):
        src = at(-k)
        copy(hop.at[2, :, share_of(me)], shift_ref.at[src], v_send.at[k], v_recv.at[src], (sec, src)).wait_recv()
        shift_out(k).wait_send()
        spread_out(k).wait_send()
        twin_out(src).wait_send()

    @pl.loop(0, half_n)
    def _(k):
        mate_out(at(2 * k + 1)).wait_send()

    @pl.loop(1, half_n)
    def _(k):
        lane_out(k).wait_send()


def per_device(value_weight, norm_gain, mask_logits, gumbel_noise, stream_in, stream_grad):
    sections = lax.axis_size("section")
    index, n = lax.axis_index("dp"), lax.axis_size("dp")
    micro, rows, width = stream_in.shape
    weight, logits, noise = value_weight[0], mask_logits[0], gumbel_noise[0]
    block, kv = weight.shape
    head = kv // VHEADS
    repeat = width // kv
    local = min(block // head, repeat)
    heads = block // (local * head)
    sharers = n * heads // VHEADS
    share = heads * head
    tokens = micro * rows
    count = n * tokens
    gain = lax.dynamic_slice_in_dim(norm_gain[0], index * block, block, 0).astype(F32)
    steps = block // head
    pattern = pl.BlockSpec((6, head // 4, kv), lambda i: (0, i, 0))
    strip = pl.BlockSpec((head, kv), lambda i: (i, 0))

    masked, core = pl.pallas_call(
        functools.partial(mask_kernel, local, head),
        grid=(steps,),
        out_shape=[jax.ShapeDtypeStruct((block, kv), BF16), jax.ShapeDtypeStruct((share, kv), BF16)],
        in_specs=[pattern, pattern, strip, pl.BlockSpec((head, 1), lambda i: (i, 0))],
        out_specs=[strip, pl.BlockSpec((head, kv), lambda i: (i // local, 0))],
        scratch_shapes=[pltpu.VMEM((head, kv), F32)],
        compiler_params=pltpu.CompilerParams(vmem_limit_bytes=LIMIT),
        name="masks",
    )(logits, noise, weight, gain[:, None])

    dma = pltpu.SemaphoreType.DMA
    vmem = pl.BlockSpec(memory_space=pltpu.VMEM)
    spread, shift, right = pl.pallas_call(
        functools.partial(relay_kernel, n, sections, sharers),
        out_shape=[
            jax.ShapeDtypeStruct((n, tokens, block), BF16),
            jax.ShapeDtypeStruct((n, tokens, share), BF16),
            jax.ShapeDtypeStruct((n, tokens, kv), BF16),
        ],
        in_specs=[vmem] * 5,
        out_specs=[vmem] * 3,
        scratch_shapes=[
            pltpu.VMEM((n, share, kv), BF16),
            pltpu.VMEM((n, tokens, kv), BF16),
            pltpu.VMEM((n // 2, tokens, kv), BF16),
            pltpu.VMEM((n // 2, tokens, kv), BF16),
            pltpu.VMEM((tokens, kv), F32),
            pltpu.VMEM((tokens, kv), F32),
            pltpu.VMEM((4, tokens, kv), BF16),
            pltpu.VMEM((tokens, kv), BF16),
            dma((n,)), dma((n,)), dma((n,)), dma((n,)), dma((n,)), dma((n,)), dma((n,)),
            dma((n,)), dma((n,)), dma((n,)), dma((n,)), dma((2,)), dma((2,)),
            dma((n,)), dma((n,)), dma((n,)), dma((n,)), dma((n,)), dma,
        ],
        compiler_params=pltpu.CompilerParams(collective_id=0, has_side_effects=True, vmem_limit_bytes=LIMIT),
        name="relay",
    )(stream_in.reshape(tokens, width), stream_grad.reshape(tokens, width), gain[None], masked, core)

    out = pl.pallas_call(
        logit_kernel,
        grid=(steps,),
        out_shape=jax.ShapeDtypeStruct(logits.shape, BF16),
        in_specs=[
            pattern,
            pattern,
            strip,
            pl.BlockSpec((1, head), lambda i: (0, i)),
            pl.BlockSpec((count, head), lambda i: (0, i)),
            pl.BlockSpec((count, head), lambda i: (0, i // local)),
            pl.BlockSpec((count, kv), lambda i: (0, 0)),
        ],
        out_specs=pattern,
        compiler_params=pltpu.CompilerParams(vmem_limit_bytes=LIMIT),
        name="logits",
    )(logits, noise, weight, gain[None], spread.reshape(count, block), shift.reshape(count, share), right.reshape(count, kv))
    return out[None]


def solution(mesh):
    return jax.shard_map(
        per_device,
        mesh=mesh,
        in_specs=(
            P("section", "dp", None),
            P("section", None),
            P("section", None, "dp", None),
            P("section", None, "dp", None),
            P(None, "dp", None),
            P(None, "dp", None),
        ),
        out_specs=P("section", None, "dp", None),
        check_vma=False,
    )
```

time: 357 us -> 163 us (0.46)
  waiting for transfers between devices: 171 us -> 0 us
  Pallas kernels: 0 us -> 159 us
  other arithmetic: 61.9 us -> 1.97 us
  local copies, waits for them, and re-layouts: 57.7 us -> 1.01 us
  matrix products: 22.1 us -> 0 us
  blocking collectives: 19 us -> 0 us
  between operations: 13.8 us -> 0.01 us
  starting transfers between devices: 8.14 us -> 0 us
    pallas_call x0 -> x3, Pallas kernels: none -> 159 us  [the longest x1 138 us: per_device(): pl.pallas_call(functools.partial(relay_kernel, n, sections, sharers), out...]
    all_gather x3 -> x0, waiting for transfers between devices: 82.2 us -> none  [the longest x1 55.4 us: per_device(): lax.all_gather(core.reshape(heads * head, kv), ('section', 'dp'), axis=0,...]
    reduce_scatter x1 -> x0, waiting for transfers between devices: 67.5 us -> none  [per_device(): first = lax.psum_scatter(part, 'dp', scatter_dimension=0, tiled=True)]
    dot_general x8 -> x0, matrix products: 22.1 us -> none  [dot(): lax.dot_general(a, b, (contract, ((), ())), preferred_element_type=F32)]
    all_to_all x1 -> x0, waiting for transfers between devices: 21.1 us -> none  [per_device(): spread = lax.all_to_all(x0, 'dp', split_axis=1, concat_axis=0, tiled=True)]
    all_to_all x1 -> x0, blocking collectives: 19 us -> none  [per_device(): shift = lax.all_to_all(mine, 'dp', split_axis=1, concat_axis=0, tiled=True)]
    convert_element_type x9 -> x2, other arithmetic: 20.7 us -> 1.97 us  [per_device(): lax.dynamic_slice_in_dim(norm_gain[0], index * block, block, 0).astype(F32)]
    reduce_sum x7 -> x0, other arithmetic: 18.6 us -> none  [the longest x1 4.73 us: per_device(): jnp.sum((masked.astype(F32) * gain[:, None]).reshape(heads, local, head,...]
  transfers between devices with their start and end apart: 5 -> 0, of which waited for: 4 -> 0; matrix products, arithmetic and copies ran while one was open for 19% -> 0% of each run, Pallas kernels for 0% -> 0%
where the time goes in v2:
time: 163 us; the launch traced here: 162 us
  Pallas kernels  159 us (98%)
  other arithmetic  1.97 us (1%)
    pallas_call x1, Pallas kernels, per_device(): pl.pallas_call(functools.partial(relay_kernel, n, sections, sharers), out...  138 us
    pallas_call x1, Pallas kernels, per_device(): pl.pallas_call(logit_kernel, grid=(steps,), out_shape=jax.ShapeDtypeStruc...  12.3 us
    pallas_call x1, Pallas kernels, per_device(): pl.pallas_call(functools.partial(mask_kernel, local, head), grid=(steps,)...  9.18 us

profile of v2, /device:TPU:0, one launch (start us, length us, event | category | flops | bytes accessed | tf_op | source)
XLA Modules:
  0.0 162.1 jit_solution(15516023181229718184)
XLA Ops:
  0.0 1.3 dynamic-slice_convert_fusion.gain_ref
  1.3 0.7 fusion
  2.0 1.0 copy.7.gain_ref
  3.0 9.2 %masks.1 = (bf16[1024,1024]{1,0:T(8,128)(2,1)}, bf16[128,1024]{1,0:T(8,128)(2,1)}) custom-call(bf16[6,256,1024]{2,1,0:T(8,128)(2,1)} %bitcast.11, bf16[6,256,1024]{2,1,0:T(8,128)(2,1)} %bitcast.13, bf16[1024,1024]{1,0:T(8,128)(2,1)} %bitcast.15, f32[1024,1]{1,0:T(8,128)} %copy.7.gain_ref), custom_call_target="tpu_custom_call" | custom-call | tf_op jit(solution)/shard_map/masks/pallas_call | solution.py:372
  12.2 137.6 %relay.1 = (bf16[8,128,1024]{2,1,0:T(8,128)(2,1)}, bf16[8,128,128]{2,1,0:T(8,128)(2,1)}, bf16[8,128,1024]{2,1,0:T(8,128)(2,1)}) custom-call(bf16[128,8192]{1,0:T(8,128)(2,1)} %bitcast.19, bf16[128,8192]{1,0:T(8,128)(2,1)} %bitcast.20, f32[1,1024]{1,0:T(1,128)} %dynamic-slice_convert_fusion.gain_ref, bf16[1024,1024]{1,0:T(8,128)(2,1)} %get-tuple-element.10.masked_ref, ...), custom_call_target="tpu_custom_call" | custom-call | tf_op jit(solution)/shard_map/relay/pallas_call | solution.py:385
  149.8 12.3 %logits.1 = bf16[6,256,1024]{2,1,0:T(8,128)(2,1)} custom-call(bf16[6,256,1024]{2,1,0:T(8,128)(2,1)} %bitcast.12, bf16[6,256,1024]{2,1,0:T(8,128)(2,1)} %bitcast.14, bf16[1024,1024]{1,0:T(8,128)(2,1)} %bitcast.16, f32[1,1024]{1,0:T(1,128)} %dynamic-slice_convert_fusion.gain_ref, bf16[1024,1024]{1,0:T(8,128)(2,1)} %bitcast.17, bf16[1024,128]{1,0:T(8,128)(2,1)} %bitcast.21, ...), custom_call_target="tpu_custom_call" | custom-call | tf_op jit(solution)/shard_map/logits/pallas_call | solution.py:411

commit v3 on v2

--- a/solution.py
+++ b/solution.py
@@ -79,7 +79,7 @@
 def relay_kernel(
     n, sections, sharers, x0_ref, top_ref, gain_ref, masked_ref, core_ref, spread_ref, shift_ref, right_ref,
     cores, parts, fromy, fromz, sums, full, hop, mine,
-    a_send, a_recv, b_send, b_recv, c_send, c_recv, d_send, y_send, y_recv, z_send, z_recv,
+    a_send, a_recv, b_send, b_recv, e_send, e_recv, p_send, p_recv, c_send, c_recv, d_send, y_send, y_recv, z_send, z_recv,
     h_send, h_recv, v_send, v_recv, g_send, g_recv, f_send, own_sem,
 ):
     me, sec = lax.axis_index("dp"), lax.axis_index("section")
@@ -92,7 +92,10 @@
     kv = masked_ref.shape[1]
     head = kv // VHEADS
     repeat = width // kv
-    half = tokens // 2
+    quarter = tokens // 4
+    across = lax.rem(sec + 2, sections)
+    beyond = lax.rem(twin + 2, sections)
+    place = me // 2
 
     def at(k):
         return lax.rem(me + k + n, n)
@@ -103,31 +106,31 @@
     def _(k):
         pl.semaphore_signal(barrier, inc=1, device_id=(sec, at(k)), device_id_type=MESH)
 
-    for step in (1, sections - 1):
+    for step in range(1, sections):
         pl.semaphore_signal(barrier, inc=1, device_id=(lax.rem(sec + step, sections), me), device_id_type=MESH)
-    pl.semaphore_wait(barrier, n + 1)
+    pl.semaphore_wait(barrier, n + sections - 2)
 
     def copy(src, dst, send, recv, where):
         return pltpu.make_async_remote_copy(
             src_ref=src, dst_ref=dst, send_sem=send, recv_sem=recv, device_id=where, device_id_type=MESH
         )
 
-    rows = pl.ds(pl.multiple_of((sec % 2) * half, half), half)
-    others = pl.ds(pl.multiple_of((1 - sec % 2) * half, half), half)
+    def quarter_of(which):
+        return pl.ds(pl.multiple_of(which * quarter, quarter), quarter)
 
     def spread_out(k):
         dest = at(k)
         cols = pl.ds(pl.multiple_of(dest * block, block), block)
+        rows = quarter_of(sec)
         return copy(x0_ref.at[rows, cols], spread_ref.at[me, rows], a_send.at[k], a_recv.at[me], (sec, dest))
 
+    def share(src, which, send, recv, to):
+        ref = spread_ref.at[src, quarter_of(which)]
+        return copy(ref, ref, send.at[src], recv.at[src], (to, me))
+
     def spread_in(src):
-        return copy(spread_ref.at[src, rows], spread_ref.at[src, rows], a_send.at[0], a_recv.at[src], (sec, mate))
-
-    def twin_out(src):
-        return copy(spread_ref.at[src, rows], spread_ref.at[src, rows], b_send.at[src], b_recv.at[src], (twin, me))
-
-    def twin_in(src):
-        return copy(spread_ref.at[src, others], spread_ref.at[src, others], b_send.at[src], b_recv.at[src], (twin, me))
+        ref = spread_ref.at[src, quarter_of(sec)]
+        return copy(ref, ref, a_send.at[0], a_recv.at[src], (sec, mate))
 
     own_cols = pl.ds(pl.multiple_of(me * block, block), block)
     own = pltpu.make_async_copy(x0_ref.at[:, own_cols], spread_ref.at[me], own_sem)
@@ -137,37 +140,70 @@
     def _(k):
         spread_out(k).start()
 
-    def gather_out(buf, send, recv, k):
-        return copy(buf.at[me], buf.at[me], send.at[k], recv.at[me], (sec, at(2 * k)))
-
-    def gather_pass(buf, send, recv, k):
-        src = at(-2 * k)
-        return copy(buf.at[src], buf.at[src], send.at[k], recv.at[src], (sec, mate))
-
-    def gather_in(buf, send, recv, src):
-        return copy(buf.at[src], buf.at[src], send.at[0], recv.at[src], (sec, mate))
+    def lane_copy(buf, send, recv, src, slot, dest):
+        return copy(buf.at[src], buf.at[src], send.at[slot], recv.at[src], (sec, dest))
+
+    def to_right(buf, send, recv, src, slot):
+        return lane_copy(buf, send, recv, src, slot, lax.rem(me + 2, n))
+
+    def to_left(buf, send, recv, src, slot):
+        return lane_copy(buf, send, recv, src, slot, lax.rem(me + n - 2, n))
+
+    def gather_pass(buf, more, recv, src):
+        return lane_copy(buf, more, recv, src, src, mate)
 
     def gather_start(buf, send, more, recv):
-        gather_pass(buf, more, recv, 0).start()
-
-        @pl.loop(1, half_n)
-        def _(k):
-            gather_out(buf, send, recv, k).start()
+        @pl.when(place < half_n - 1)
+        def _():
+            to_right(buf, send, recv, me, me).start()
+
+        @pl.when(place > 0)
+        def _():
+            to_left(buf, send, recv, me, mate).start()
+
+        gather_pass(buf, more, recv, me).start()
 
     def gather_forward(buf, send, more, recv, k):
-        gather_in(buf, send, recv, at(-2 * k)).wait_recv()
-        gather_pass(buf, more, recv, k).start()
+        @pl.when(place >= k)
+        def _():
+            src = me - 2 * k
+            gather_pass(buf, more, recv, src).wait_recv()
+
+            @pl.when(place < half_n - 1)
+            def _():
+                to_right(buf, send, recv, src, src).start()
+
+            gather_pass(buf, more, recv, src).start()
+
+        @pl.when(place + k < half_n)
+        def _():
+            src = me + 2 * k
+            gather_pass(buf, more, recv, src).wait_recv()
+
+            @pl.when(place > 0)
+            def _():
+                to_left(buf, send, recv, src, src).start()
+
+            gather_pass(buf, more, recv, src).start()
 
     def gather_end(buf, send, more, recv):
         @pl.loop(0, half_n)
         def _(k):
-            pair = at(-2 * k)
-            gather_in(buf, send, recv, pair + 1 - 2 * lane).wait_recv()
-            gather_pass(buf, more, recv, k).wait_send()
-
-        @pl.loop(1, half_n)
-        def _(k):
-            gather_out(buf, send, recv, k).wait_send()
+            src = 2 * k + lane
+            gather_pass(buf, more, recv, 2 * k + 1 - lane).wait_recv()
+            gather_pass(buf, more, recv, src).wait_send()
+
+            @pl.when((k <= place) & (place < half_n - 1))
+            def _():
+                to_right(buf, send, recv, src, src).wait_send()
+
+            @pl.when((k > place) & (place > 0))
+            def _():
+                to_left(buf, send, recv, src, src).wait_send()
+
+        @pl.when(place > 0)
+        def _():
+            to_left(buf, send, recv, me, mate).wait_send()
 
     cores[me] = core_ref[...]
     gather_start(cores, c_send, d_send, c_recv)
@@ -185,21 +221,36 @@
     def arrive(k):
         src = at(-k)
         spread_in(src).wait_recv()
-        twin_out(src).start()
+        share(src, sec, e_send, e_recv, across).start()
+        share(src, sec, b_send, b_recv, twin).start()
+
+    def cross(k):
+        src = at(-k)
+        share(src, across, e_send, e_recv, across).wait_recv()
+        share(src, across, p_send, p_recv, twin).start()
 
     def whole(k):
         src = at(-k)
-        twin_in(src).wait_recv()
+        share(src, twin, b_send, b_recv, twin).wait_recv()
+        share(src, beyond, p_send, p_recv, twin).wait_recv()
         product(src)
 
     arrive(1)
+    arrive(2)
+    cross(1)
 
     @pl.loop(1, half_n)
     def _(j):
-        arrive(2 * j)
+        arrive(2 * j + 1)
+        cross(2 * j)
         whole(2 * j - 1)
         mate_out(at(1 - 2 * j)).start()
-        arrive(2 * j + 1)
+
+        @pl.when(j < half_n - 1)
+        def _():
+            arrive(2 * j + 2)
+
+        cross(2 * j + 1)
         whole(2 * j)
         gather_forward(cores, c_send, d_send, c_recv, j)
 
@@ -281,10 +332,10 @@
     def _():
         copy(mine, hop.at[2], h_send.at[0], h_recv.at[0], (up, me)).start()
 
-    share = shift_ref.shape[2]
+    part = shift_ref.shape[2]
 
     def share_of(dest):
-        return pl.ds(pl.multiple_of((dest // sharers) * share, share), share)
+        return pl.ds(pl.multiple_of((dest // sharers) * part, part), part)
 
     def shift_out(k):
         dest = at(k)
@@ -339,7 +390,9 @@
         copy(hop.at[2, :, share_of(me)], shift_ref.at[src], v_send.at[k], v_recv.at[src], (sec, src)).wait_recv()
         shift_out(k).wait_send()
         spread_out(k).wait_send()
-        twin_out(src).wait_send()
+        share(src, sec, b_send, b_recv, twin).wait_send()
+        share(src, sec, e_send, e_recv, across).wait_send()
+        share(src, across, p_send, p_recv, twin).wait_send()
 
     @pl.loop(0, half_n)
     def _(k):
@@ -401,6 +454,7 @@
             pltpu.VMEM((4, tokens, kv), BF16),
             pltpu.VMEM((tokens, kv), BF16),
             dma((n,)), dma((n,)), dma((n,)), dma((n,)), dma((n,)), dma((n,)), dma((n,)),
+            dma((n,)), dma((n,)), dma((n,)), dma((n,)),
             dma((n,)), dma((n,)), dma((n,)), dma((n,)), dma((2,)), dma((2,)),
             dma((n,)), dma((n,)), dma((n,)), dma((n,)), dma((n,)), dma,
         ],

time: 163 us -> 142 us (0.87)
  Pallas kernels: 159 us -> 138 us
    pallas_call x1, Pallas kernels: 138 us -> 117 us  [per_device(): pl.pallas_call(functools.partial(relay_kernel, n, sections, sharers), out...]
where the time goes in v3:
time: 142 us; the launch traced here: 141 us
  Pallas kernels  138 us (97%)
  other arithmetic  1.97 us (1%)
    pallas_call x1, Pallas kernels, per_device(): pl.pallas_call(functools.partial(relay_kernel, n, sections, sharers), out...  117 us
    pallas_call x1, Pallas kernels, per_device(): pl.pallas_call(logit_kernel, grid=(steps,), out_shape=jax.ShapeDtypeStruc...  12.3 us
    pallas_call x1, Pallas kernels, per_device(): pl.pallas_call(functools.partial(mask_kernel, local, head), grid=(steps,)...  9.18 us

profile of v3, /device:TPU:0, one launch (start us, length us, event | category | flops | bytes accessed | tf_op | source)
XLA Modules:
  0.0 141.0 jit_solution(4478661886452903529)
XLA Ops:
  0.0 1.3 dynamic-slice_convert_fusion.gain_ref
  1.3 0.7 fusion
  2.0 1.0 copy.7.gain_ref
  3.0 9.2 %masks.1 = (bf16[1024,1024]{1,0:T(8,128)(2,1)}, bf16[128,1024]{1,0:T(8,128)(2,1)}) custom-call(bf16[6,256,1024]{2,1,0:T(8,128)(2,1)} %bitcast.11, bf16[6,256,1024]{2,1,0:T(8,128)(2,1)} %bitcast.13, bf16[1024,1024]{1,0:T(8,128)(2,1)} %bitcast.15, f32[1024,1]{1,0:T(8,128)} %copy.7.gain_ref), custom_call_target="tpu_custom_call" | custom-call | tf_op jit(solution)/shard_map/masks/pallas_call | solution.py:425
  12.2 116.5 %relay.1 = (bf16[8,128,1024]{2,1,0:T(8,128)(2,1)}, bf16[8,128,128]{2,1,0:T(8,128)(2,1)}, bf16[8,128,1024]{2,1,0:T(8,128)(2,1)}) custom-call(bf16[128,8192]{1,0:T(8,128)(2,1)} %bitcast.19, bf16[128,8192]{1,0:T(8,128)(2,1)} %bitcast.20, f32[1,1024]{1,0:T(1,128)} %dynamic-slice_convert_fusion.gain_ref, bf16[1024,1024]{1,0:T(8,128)(2,1)} %get-tuple-element.10.masked_ref, ...), custom_call_target="tpu_custom_call" | custom-call | tf_op jit(solution)/shard_map/relay/pallas_call | solution.py:438
  128.7 12.3 %logits.1 = bf16[6,256,1024]{2,1,0:T(8,128)(2,1)} custom-call(bf16[6,256,1024]{2,1,0:T(8,128)(2,1)} %bitcast.12, bf16[6,256,1024]{2,1,0:T(8,128)(2,1)} %bitcast.14, bf16[1024,1024]{1,0:T(8,128)(2,1)} %bitcast.16, f32[1,1024]{1,0:T(1,128)} %dynamic-slice_convert_fusion.gain_ref, bf16[1024,1024]{1,0:T(8,128)(2,1)} %bitcast.17, bf16[1024,128]{1,0:T(8,128)(2,1)} %bitcast.21, ...), custom_call_target="tpu_custom_call" | custom-call | tf_op jit(solution)/shard_map/logits/pallas_call | solution.py:465

commit v4 on v3

--- a/solution.py
+++ b/solution.py
@@ -37,27 +37,28 @@
     return [score * inverse for score in scores]
 
 
-def mask_kernel(local, head, logits_ref, noise_ref, weight_ref, gain_ref, masked_ref, core_ref, total):
-    size = weight_ref.shape[0]
-    groups = size // 4
-    order = planar(size)
-    p = pattern_probs(logits_ref, noise_ref)
+def mask_step(step, head, local, logits_ref, noise_ref, weight_ref, gain_ref, masked_ref, core_ref, total):
+    groups = head // 4
+    rows = pl.ds(pl.multiple_of(step * head, head), head)
+    some = pl.ds(pl.multiple_of(step * groups, groups), groups)
+    order = planar(head)
+    p = pattern_probs(logits_ref.at[:, some], noise_ref.at[:, some])
     planes = [p[0] + p[1] + p[2], p[0] + p[3] + p[4], p[1] + p[3] + p[5], p[2] + p[4] + p[5]]
-    apart = dot(order, weight_ref[...], ((0,), (0,)))
-    rows = [(apart[r * groups:(r + 1) * groups] * planes[r]).astype(BF16) for r in range(4)]
-    masked = dot(order, jnp.concatenate(rows, axis=0), ((1,), (0,)))
-    masked_ref[...] = masked.astype(BF16)
-    term = masked * gain_ref[...]
-
-    @pl.when(pl.program_id(0) % local == 0)
+    apart = dot(order, weight_ref[rows], ((0,), (0,)))
+    kept = [(apart[r * groups:(r + 1) * groups] * planes[r]).astype(BF16) for r in range(4)]
+    masked = dot(order, jnp.concatenate(kept, axis=0), ((1,), (0,)))
+    masked_ref[rows] = masked.astype(BF16)
+    term = masked * gain_ref[rows]
+
+    @pl.when(step % local == 0)
     def _():
         total[...] = term
 
-    @pl.when(pl.program_id(0) % local != 0)
+    @pl.when(step % local != 0)
     def _():
         total[...] += term
 
-    core_ref[...] = total[...].astype(BF16)
+    core_ref[pl.ds(pl.multiple_of((step // local) * head, head), head)] = total[...].astype(BF16)
 
 
 def logit_kernel(logits_ref, noise_ref, weight_ref, gain_ref, spread_ref, shift_ref, right_ref, out_ref):
@@ -77,8 +78,8 @@
 
 
 def relay_kernel(
-    n, sections, sharers, x0_ref, top_ref, gain_ref, masked_ref, core_ref, spread_ref, shift_ref, right_ref,
-    cores, parts, fromy, fromz, sums, full, hop, mine,
+    n, sections, sharers, local, x0_ref, top_ref, gain_ref, logits_ref, noise_ref, weight_ref, column_ref,
+    spread_ref, shift_ref, right_ref, masked_ref, running, cores, parts, fromy, fromz, sums, full, hop, mine,
     a_send, a_recv, b_send, b_recv, e_send, e_recv, p_send, p_recv, c_send, c_recv, d_send, y_send, y_recv, z_send, z_recv,
     h_send, h_recv, v_send, v_recv, g_send, g_recv, f_send, own_sem,
 ):
@@ -205,7 +206,12 @@
         def _():
             to_left(buf, send, recv, me, mate).wait_send()
 
-    cores[me] = core_ref[...]
+    head_steps = block // head
+
+    @pl.loop(0, head_steps)
+    def _(step):
+        mask_step(step, head, local, logits_ref, noise_ref, weight_ref, column_ref, masked_ref, cores.at[me], running)
+
     gather_start(cores, c_send, d_send, c_recv)
 
     def product(src):
@@ -236,28 +242,10 @@
         product(src)
 
     arrive(1)
+    own.wait()
+    product(me)
     arrive(2)
     cross(1)
-
-    @pl.loop(1, half_n)
-    def _(j):
-        arrive(2 * j + 1)
-        cross(2 * j)
-        whole(2 * j - 1)
-        mate_out(at(1 - 2 * j)).start()
-
-        @pl.when(j < half_n - 1)
-        def _():
-            arrive(2 * j + 2)
-
-        cross(2 * j + 1)
-        whole(2 * j)
-        gather_forward(cores, c_send, d_send, c_recv, j)
-
-    whole(n - 1)
-    mate_out(at(1 - n)).start()
-    own.wait()
-    product(me)
 
     folded = []
     tops = []
@@ -278,6 +266,24 @@
     sums[...] = jnp.concatenate(folded, axis=1)
     hop[0] = jnp.concatenate(tops, axis=1).astype(BF16)
 
+    @pl.loop(1, half_n)
+    def _(j):
+        arrive(2 * j + 1)
+        cross(2 * j)
+        whole(2 * j - 1)
+        mate_out(at(1 - 2 * j)).start()
+
+        @pl.when(j < half_n - 1)
+        def _():
+            arrive(2 * j + 2)
+
+        cross(2 * j + 1)
+        whole(2 * j)
+        gather_forward(cores, c_send, d_send, c_recv, j)
+
+    whole(n - 1)
+    mate_out(at(1 - n)).start()
+
     def lane_out(k):
         owner = at(2 * k)
         return copy(parts.at[owner], fromz.at[me // 2], z_send.at[k], z_recv.at[me // 2], (sec, owner))
@@ -345,8 +351,8 @@
     def _(k):
         shift_out(k).start()
 
-    local = pltpu.make_async_copy(hop.at[2, :, share_of(me)], shift_ref.at[me], own_sem)
-    local.start()
+    stay = pltpu.make_async_copy(hop.at[2, :, share_of(me)], shift_ref.at[me], own_sem)
+    stay.start()
 
     @pl.when(sec == sections - 1)
     def _():
@@ -374,7 +380,7 @@
         gather_forward(right_ref, g_send, f_send, g_recv, k)
 
     gather_end(right_ref, g_send, f_send, g_recv)
-    local.wait()
+    stay.wait()
 
     @pl.when(sec < sections - 1)
     def _():
@@ -422,29 +428,20 @@
     pattern = pl.BlockSpec((6, head // 4, kv), lambda i: (0, i, 0))
     strip = pl.BlockSpec((head, kv), lambda i: (i, 0))
 
-    masked, core = pl.pallas_call(
-        functools.partial(mask_kernel, local, head),
-        grid=(steps,),
-        out_shape=[jax.ShapeDtypeStruct((block, kv), BF16), jax.ShapeDtypeStruct((share, kv), BF16)],
-        in_specs=[pattern, pattern, strip, pl.BlockSpec((head, 1), lambda i: (i, 0))],
-        out_specs=[strip, pl.BlockSpec((head, kv), lambda i: (i // local, 0))],
-        scratch_shapes=[pltpu.VMEM((head, kv), F32)],
-        compiler_params=pltpu.CompilerParams(vmem_limit_bytes=LIMIT),
-        name="masks",
-    )(logits, noise, weight, gain[:, None])
-
     dma = pltpu.SemaphoreType.DMA
     vmem = pl.BlockSpec(memory_space=pltpu.VMEM)
     spread, shift, right = pl.pallas_call(
-        functools.partial(relay_kernel, n, sections, sharers),
+        functools.partial(relay_kernel, n, sections, sharers, local),
         out_shape=[
             jax.ShapeDtypeStruct((n, tokens, block), BF16),
             jax.ShapeDtypeStruct((n, tokens, share), BF16),
             jax.ShapeDtypeStruct((n, tokens, kv), BF16),
         ],
-        in_specs=[vmem] * 5,
+        in_specs=[vmem] * 7,
         out_specs=[vmem] * 3,
         scratch_shapes=[
+            pltpu.VMEM((block, kv), BF16),
+            pltpu.VMEM((head, kv), F32),
             pltpu.VMEM((n, share, kv), BF16),
             pltpu.VMEM((n, tokens, kv), BF16),
             pltpu.VMEM((n // 2, tokens, kv), BF16),
@@ -460,7 +457,7 @@
         ],
         compiler_params=pltpu.CompilerParams(collective_id=0, has_side_effects=True, vmem_limit_bytes=LIMIT),
         name="relay",
-    )(stream_in.reshape(tokens, width), stream_grad.reshape(tokens, width), gain[None], masked, core)
+    )(stream_in.reshape(tokens, width), stream_grad.reshape(tokens, width), gain[None], logits, noise, weight, gain[:, None])
 
     out = pl.pallas_call(
         logit_kernel,

time: 142 us -> 135 us (0.951)
  Pallas kernels: 138 us -> 132 us
    pallas_call x2 -> x1, Pallas kernels: 126 us -> 119 us  [per_device(): pl.pallas_call(functools.partial(relay_kernel, n, sections, sharers, loca...]
where the time goes in v4:
time: 135 us
  Pallas kernels  132 us (98%)
  other arithmetic  1.97 us (1%)
    pallas_call x1, Pallas kernels, per_device(): pl.pallas_call(functools.partial(relay_kernel, n, sections, sharers, loca...  119 us
    pallas_call x1, Pallas kernels, per_device(): pl.pallas_call(logit_kernel, grid=(steps,), out_shape=jax.ShapeDtypeStruc...  12.3 us

profile of v4, /device:TPU:0, one launch (start us, length us, event | category | flops | bytes accessed | tf_op | source)
XLA Modules:
  0.0 134.5 jit_solution(433190546286988978)
XLA Ops:
  0.0 1.3 dynamic-slice_convert_fusion.gain_ref
  1.3 0.7 fusion
  2.0 1.0 copy.7.column_ref
  3.0 119.3 %relay.1 = (bf16[8,128,1024]{2,1,0:T(8,128)(2,1)}, bf16[8,128,128]{2,1,0:T(8,128)(2,1)}, bf16[8,128,1024]{2,1,0:T(8,128)(2,1)}) custom-call(bf16[128,8192]{1,0:T(8,128)(2,1)} %bitcast.19, bf16[128,8192]{1,0:T(8,128)(2,1)} %bitcast.20, f32[1,1024]{1,0:T(1,128)} %dynamic-slice_convert_fusion.gain_ref, bf16[6,256,1024]{2,1,0:T(8,128)(2,1)} %bitcast.11, ...), custom_call_target="tpu_custom_call" | custom-call | tf_op jit(solution)/shard_map/relay/pallas_call | solution.py:433
  122.3 12.3 %logits.1 = bf16[6,256,1024]{2,1,0:T(8,128)(2,1)} custom-call(bf16[6,256,1024]{2,1,0:T(8,128)(2,1)} %bitcast.12, bf16[6,256,1024]{2,1,0:T(8,128)(2,1)} %bitcast.14, bf16[1024,1024]{1,0:T(8,128)(2,1)} %bitcast.16, f32[1,1024]{1,0:T(1,128)} %dynamic-slice_convert_fusion.gain_ref, bf16[1024,1024]{1,0:T(8,128)(2,1)} %bitcast.17, bf16[1024,128]{1,0:T(8,128)(2,1)} %bitcast.21, ...), custom_call_target="tpu_custom_call" | custom-call | tf_op jit(solution)/shard_map/logits/pallas_call | solution.py:462

commit v5 on v4

--- a/solution.py
+++ b/solution.py
@@ -61,25 +61,29 @@
     core_ref[pl.ds(pl.multiple_of((step // local) * head, head), head)] = total[...].astype(BF16)
 
 
-def logit_kernel(logits_ref, noise_ref, weight_ref, gain_ref, spread_ref, shift_ref, right_ref, out_ref):
-    size = weight_ref.shape[0]
-    groups = size // 4
-    order = planar(size)
-    left = (spread_ref[...].astype(F32) + shift_ref[...].astype(F32)) * gain_ref[...]
+def logit_step(step, head, local, logits_ref, noise_ref, weight_ref, gain_ref, spread_ref, shift_ref, right_ref, out_ref):
+    groups = head // 4
+    n, tokens, kv = right_ref.shape
+    rows = pl.ds(pl.multiple_of(step * head, head), head)
+    some = pl.ds(pl.multiple_of(step * groups, groups), groups)
+    mine = pl.ds(pl.multiple_of((step // local) * head, head), head)
+    order = planar(head)
+    left = spread_ref[:, :, rows].astype(F32) + shift_ref[:, :, mine].astype(F32)
+    left = left.reshape(n * tokens, head) * gain_ref[:, rows]
     left = dot(left.astype(BF16), order, ((1,), (0,))).astype(BF16)
-    wgrad = dot(left, right_ref[...], ((0,), (0,)))
-    grad = wgrad * dot(order, weight_ref[...], ((0,), (0,)))
+    wgrad = dot(left, right_ref[...].reshape(n * tokens, kv), ((0,), (0,)))
+    grad = wgrad * dot(order, weight_ref[rows], ((0,), (0,)))
     a, b, c, d = [grad[r * groups:(r + 1) * groups] for r in range(4)]
-    p = pattern_probs(logits_ref, noise_ref)
+    p = pattern_probs(logits_ref.at[:, some], noise_ref.at[:, some])
     dprob = [a + b, a + c, a + d, b + c, b + d, c + d]
     mean = sum(p[k] * dprob[k] for k in range(6))
     for k in range(6):
-        out_ref[k] = (p[k] * (dprob[k] - mean) / sharpness_divisor).astype(BF16)
+        out_ref[k, some] = (p[k] * (dprob[k] - mean) / sharpness_divisor).astype(BF16)
 
 
 def relay_kernel(
     n, sections, sharers, local, x0_ref, top_ref, gain_ref, logits_ref, noise_ref, weight_ref, column_ref,
-    spread_ref, shift_ref, right_ref, masked_ref, running, cores, parts, fromy, fromz, sums, full, hop, mine,
+    out_ref, spread_ref, shift_ref, right_ref, masked_ref, running, cores, parts, fromy, fromz, sums, full, hop, mine,
     a_send, a_recv, b_send, b_recv, e_send, e_recv, p_send, p_recv, c_send, c_recv, d_send, y_send, y_recv, z_send, z_recv,
     h_send, h_recv, v_send, v_recv, g_send, g_recv, f_send, own_sem,
 ):
@@ -408,6 +412,12 @@
     def _(k):
         lane_out(k).wait_send()
 
+    @pl.loop(0, head_steps)
+    def _(step):
+        logit_step(
+            step, head, local, logits_ref, noise_ref, weight_ref, gain_ref, spread_ref, shift_ref, right_ref, out_ref
+        )
+
 
 def per_device(value_weight, norm_gain, mask_logits, gumbel_noise, stream_in, stream_grad):
     sections = lax.axis_size("section")
@@ -422,24 +432,19 @@
     sharers = n * heads // VHEADS
     share = heads * head
     tokens = micro * rows
-    count = n * tokens
     gain = lax.dynamic_slice_in_dim(norm_gain[0], index * block, block, 0).astype(F32)
-    steps = block // head
-    pattern = pl.BlockSpec((6, head // 4, kv), lambda i: (0, i, 0))
-    strip = pl.BlockSpec((head, kv), lambda i: (i, 0))
 
     dma = pltpu.SemaphoreType.DMA
     vmem = pl.BlockSpec(memory_space=pltpu.VMEM)
-    spread, shift, right = pl.pallas_call(
+    out = pl.pallas_call(
         functools.partial(relay_kernel, n, sections, sharers, local),
-        out_shape=[
-            jax.ShapeDtypeStruct((n, tokens, block), BF16),
-            jax.ShapeDtypeStruct((n, tokens, share), BF16),
-            jax.ShapeDtypeStruct((n, tokens, kv), BF16),
-        ],
+        out_shape=jax.ShapeDtypeStruct(logits.shape, BF16),
         in_specs=[vmem] * 7,
-        out_specs=[vmem] * 3,
+        out_specs=vmem,
         scratch_shapes=[
+            pltpu.VMEM((n, tokens, block), BF16),
+            pltpu.VMEM((n, tokens, share), BF16),
+            pltpu.VMEM((n, tokens, kv), BF16),
             pltpu.VMEM((block, kv), BF16),
             pltpu.VMEM((head, kv), F32),
             pltpu.VMEM((n, share, kv), BF16),
@@ -459,23 +464,6 @@
         name="relay",
     )(stream_in.reshape(tokens, width), stream_grad.reshape(tokens, width), gain[None], logits, noise, weight, gain[:, None])
 
-    out = pl.pallas_call(
-        logit_kernel,
-        grid=(steps,),
-        out_shape=jax.ShapeDtypeStruct(logits.shape, BF16),
-        in_specs=[
-            pattern,
-            pattern,
-            strip,
-            pl.BlockSpec((1, head), lambda i: (0, i)),
-            pl.BlockSpec((count, head), lambda i: (0, i)),
-            pl.BlockSpec((count, head), lambda i: (0, i // local)),
-            pl.BlockSpec((count, kv), lambda i: (0, 0)),
-        ],
-        out_specs=pattern,
-        compiler_params=pltpu.CompilerParams(vmem_limit_bytes=LIMIT),
-        name="logits",
-    )(logits, noise, weight, gain[None], spread.reshape(count, block), shift.reshape(count, share), right.reshape(count, kv))
     return out[None]
 
 

time: 135 us -> 134 us (level)
  Pallas kernels: 132 us -> 127 us
  local copies, waits for them, and re-layouts: 1.03 us -> 5.16 us
    pallas_call x1 -> x0, Pallas kernels: 12.3 us -> none  [per_device(): pl.pallas_call(logit_kernel, grid=(steps,), out_shape=jax.ShapeDtypeStruc...]
    pallas_call x1, Pallas kernels: 119 us -> 127 us  [per_device(): pl.pallas_call(functools.partial(relay_kernel, n, sections, sharers, loca...]
    unnamed x0 -> x1, local copies, waits for them, and re-layouts: none -> 4.13 us
where the time goes in v5:
time: 134 us
  Pallas kernels  127 us (95%)
  local copies, waits for them, and re-layouts  5.16 us (4%)
  other arithmetic  1.98 us (1%)
    pallas_call x1, Pallas kernels, per_device(): pl.pallas_call(functools.partial(relay_kernel, n, sections, sharers, loca...  127 us
    unnamed x1, local copies, waits for them, and re-layouts  4.13 us

profile of v5, /device:TPU:0, one launch (start us, length us, event | category | flops | bytes accessed | tf_op | source)
XLA Modules:
  0.0 133.7 jit_solution(17997001051441993345)
XLA Ops:
  0.0 0.7 fusion
  0.7 1.3 dynamic-slice_convert_fusion.gain_ref
  2.0 1.0 copy.7.column_ref
  3.0 126.5 %relay.1 = bf16[6,256,1024]{2,1,0:T(8,128)(2,1)} custom-call(bf16[128,8192]{1,0:T(8,128)(2,1)} %bitcast.11, bf16[128,8192]{1,0:T(8,128)(2,1)} %bitcast.12, f32[1,1024]{1,0:T(1,128)} %dynamic-slice_convert_fusion.gain_ref, bf16[6,256,1024]{2,1,0:T(8,128)(2,1)} %bitcast.9, bf16[6,256,1024]{2,1,0:T(8,128)(2,1)} %bitcast.10, bf16[1024,1024]{1,0:T(8,128)(2,1)} %bitcast.13, ...), custom_call_target="tpu_custom_call" | custom-call | tf_op jit(solution)/shard_map/relay/pallas_call | solution.py:439
  129.6 4.1 %copy.9 = bf16[1,6,256,1024]{3,2,1,0:T(8,128)(2,1)} copy(bf16[1,6,256,1024]{3,2,1,0:T(8,128)(2,1)} %bitcast.8) | data formatting | bytes 6291456
